TPU v7x, 128 devices: a whole 4x4x4 slice. The times are simulated.
128 devices in a mesh: cut: 16 (over y, x), depth: 8 (over z, core).
Axes of the slice: x: 4, y: 4, z: 4, core: 2. Of those that a mesh axis runs over, the one named last changes fastest.
Arguments:
- initial_state: float32 [9, 256, 128, 128], P(None, 'cut', 'depth'), may hold values from -6 to 6
- density: float32 [256, 128, 128], P('cut', 'depth'), may hold values from 0.5 to 2
- yield_flags: int32 [256, 128], P('cut', 'depth'), may hold values 0 or 1
- yield_stress: float32 [256, 128], P('cut', 'depth'), may hold values from 0.5 to 4
- crossing_weights: bfloat16 [65536, 128, 128], P(('cut', 'depth')), may hold values from 0.0029907227 to 0.099609375
- new_owner: int32 [65536, 1], P(('cut', 'depth')), may hold values from 0 to 127; in each aligned block of 512 rows (0 to 511, 512 to 1023, ...) at most 6 rows name the same one
- new_slot: int32 [65536], P(('cut', 'depth')), may hold values from 0 to 255
Outputs:
- state_after: float32 [9, 256, 128, 128], P(None, 'cut', 'depth')
- new_integrals: float32 [32768, 9, 128], P(('cut', 'depth'))
Inputs may be any that keep to these rules, and one draw needn't show every extreme that they name: `new_owner`: among the 512 pairs of one device, at most 6 name the same owner, a bound that some block reaches of them.
All inputs are finite; a program needn't handle non-finite values. No bound on the sum of `yield_flags` on one device may be relied on, other than what follows from the above.
Results may differ from a plain program's by a relative error of at most 0.003.
Values sent between devices are 32-bit elements; how exact they have to be, the bound alone decides.
No kernel may reach another device: no remote copies, remote signals or barrier semaphores. Data moves between devices by JAX's collectives and lax.ppermute only.
A program may use at most 128 MiB of HBM per device.

v0:
```python
import jax
import jax.numpy as jnp
from jax import lax
from jax.sharding import PartitionSpec as P

time_step = 0.15
lame_first = 1.0
shear_modulus = 0.6


def with_halo(block, sides, width):
    for axis, dim in sides:
        count = lax.axis_size(axis)
        forward = [(i, i + 1) for i in range(count - 1)]
        backward = [(target, source) for source, target in forward]
        low = lax.ppermute(
            lax.slice_in_dim(block, block.shape[dim] - width, None, axis=dim), axis, forward
        )
        high = lax.ppermute(lax.slice_in_dim(block, 0, width, axis=dim), axis, backward)
        block = jnp.concatenate([low, block, high], axis=dim)
    return block


def spread(values, along_axis):
    if along_axis == 1:
        return 0.5 * (values[:, 2:, 1:-1] - values[:, :-2, 1:-1])
    if along_axis == 2:
        return 0.5 * (values[:, 1:-1, 2:] - values[:, 1:-1, :-2])
    inner = values[:, 1:-1, 1:-1]
    padded = jnp.pad(inner, ((0, 0), (0, 0), (0, 0), (1, 1)))
    return 0.5 * (padded[..., 2:] - padded[..., :-2])


def divergence_of(grads):
    return jnp.stack(
        [
            grads[0][0] + grads[1][3] + grads[2][5],
            grads[0][3] + grads[1][1] + grads[2][4],
            grads[0][5] + grads[1][4] + grads[2][2],
        ]
    )


def plastic_return(stress, grads, yield_flags, yield_stress):
    strain_rate = [
        grads[0][0],
        grads[1][1],
        grads[2][2],
        0.5 * (grads[1][0] + grads[0][1]),
        0.5 * (grads[2][1] + grads[1][2]),
        0.5 * (grads[2][0] + grads[0][2]),
    ]
    trace_rate = strain_rate[0] + strain_rate[1] + strain_rate[2]
    trial_stress = []
    for component in range(6):
        update = 2.0 * shear_modulus * strain_rate[component]
        if component < 3:
            update = update + lame_first * trace_rate
        trial_stress.append(stress[component] + time_step * update)
    pressure = (trial_stress[0] + trial_stress[1] + trial_stress[2]) / 3.0
    deviator = [
        trial_stress[0] - pressure,
        trial_stress[1] - pressure,
        trial_stress[2] - pressure,
        trial_stress[3],
        trial_stress[4],
        trial_stress[5],
    ]
    equivalent = jnp.sqrt(
        1.5
        * (
            deviator[0] ** 2
            + deviator[1] ** 2
            + deviator[2] ** 2
            + 2.0 * (deviator[3] ** 2 + deviator[4] ** 2 + deviator[5] ** 2)
        )
    )
    limit = yield_stress[:, :, None]
    factor = jnp.where(yield_flags[:, :, None] == 1, limit / jnp.maximum(equivalent, limit), 1.0)
    return jnp.stack(
        [
            pressure + factor * deviator[0],
            pressure + factor * deviator[1],
            pressure + factor * deviator[2],
            factor * deviator[3],
            factor * deviator[4],
            factor * deviator[5],
        ]
    )


def velocity_update(stress_ext, velocity_inner, inverse_inner):
    grads = [spread(stress_ext, 1), spread(stress_ext, 2), spread(stress_ext, 3)]
    return velocity_inner + time_step * divergence_of(grads) * inverse_inner


def stress_update(velocity_ext, stress_own, yield_flags, yield_stress):
    grads = [spread(velocity_ext, 1), spread(velocity_ext, 2), spread(velocity_ext, 3)]
    return plastic_return(stress_own, grads, yield_flags, yield_stress)


def on_device(
    initial_state, density, yield_flags, yield_stress, crossing_weights, new_owner, new_slot
):
    inverse_density = 1.0 / density
    velocity_field = initial_state[:3]
    stress = initial_state[3:]
    for turn_index in range(2):
        stress_ext = with_halo(stress, (("cut", 1), ("depth", 2)), 1)
        velocity_field = velocity_update(stress_ext, velocity_field, inverse_density)
        velocity_ext = with_halo(velocity_field, (("cut", 1), ("depth", 2)), 1)
        stress = stress_update(velocity_ext, stress, yield_flags, yield_stress)
    state_after = jnp.concatenate([velocity_field, stress], 0)
    width = state_after.shape[3]
    old_count = state_after.shape[1] * state_after.shape[2]
    pair_count = new_owner.shape[0]
    crossings = pair_count // old_count
    fields = state_after.astype(jnp.bfloat16).reshape(9, old_count, width)
    weight_blocks = crossing_weights.reshape(old_count, crossings, width, width)
    contribution = jnp.einsum(
        "cbi,boij->bocj", fields, weight_blocks, preferred_element_type=jnp.float32
    )
    contribution = contribution.reshape(pair_count, 9 * width)
    cut_count = lax.axis_size("cut")
    depth_count = lax.axis_size("depth")
    devices = cut_count * depth_count
    capacity = max(2, 3 * pair_count // (2 * devices))
    owners = new_owner[:, 0]
    owner_hits = (owners[:, None] == jnp.arange(devices, dtype=jnp.int32)[None, :]).astype(
        jnp.int32
    )
    earlier = jnp.cumsum(owner_hits, 0) - owner_hits
    slot_rank = jnp.sum(earlier * owner_hits, 1)
    position = owners * capacity + slot_rank
    placing = (
        jnp.arange(devices * capacity, dtype=jnp.int32)[:, None] == position[None, :]
    ).astype(jnp.float32)
    outgoing = jnp.dot(
        placing, contribution, precision=lax.Precision.HIGHEST, preferred_element_type=jnp.float32
    ).reshape(devices * capacity, 9, width)
    labels = jnp.dot(
        placing,
        new_slot.astype(jnp.float32),
        precision=lax.Precision.HIGHEST,
        preferred_element_type=jnp.float32,
    )
    arrived, arrived_labels = (
        lax.all_to_all(outgoing, ("cut", "depth"), split_axis=0, concat_axis=0, tiled=True),
        lax.all_to_all(labels, ("cut", "depth"), split_axis=0, concat_axis=0, tiled=True),
    )
    arrived = arrived.reshape(devices * capacity, 9 * width)
    targets = arrived_labels.astype(jnp.int32)
    gathering = (jnp.arange(old_count, dtype=jnp.int32)[:, None] == targets[None, :]).astype(
        jnp.float32
    )
    new_integrals = jnp.dot(
        gathering, arrived, precision=lax.Precision.HIGHEST, preferred_element_type=jnp.float32
    ).reshape(old_count, 9, width)
    return (state_after, new_integrals)


def solution(mesh):
    return jax.shard_map(
        on_device,
        mesh=mesh,
        in_specs=(
            P(None, "cut", "depth", None),
            P("cut", "depth", None),
            P("cut", "depth"),
            P("cut", "depth"),
            P(("cut", "depth"), None, None),
            P(("cut", "depth"), None),
            P(("cut", "depth")),
        ),
        out_specs=(P(None, "cut", "depth", None), P(("cut", "depth"), None, None)),
        check_vma=False,
    )
```

profile of v0, /device:TPU:1, one launch (start us, length us, event | category | flops | bytes accessed | tf_op | source)
XLA Modules:
  0.0 211.0 jit_solution(11894011556675884732)
XLA Ops:
  0.6 0.8 fusion.71
  1.5 3.9 %collective-permute-start.1 = (f32[6,1,16,128]{3,2,1,0:T(8,128)S(1)}, f32[6,1,16,128]{3,2,1,0:T(8,128)S(1)}, u32[]{:S(2)}, u32[]{:S(2)}) collective-permute-start(f32[6,1,16,128]{3,2,1,0:T(8,128)S(1)} %get-tuple-element.40), channel_id=1, source_target_pairs={{0,8},{8,16},{16,24},{24,32},{32,40},{40,48},{48,56},{56,64},{64,7... | collective-permute-start | bytes 147464 | tf_op jit(solution)/shard_map/ppermute | solution.py:16
  5.4 1.3 collective-permute-start
  6.7 0.8 copy.34
  7.5 0.2 fusion.42
  7.7 1.2 slice.283
  9.0 1.3 collective-permute-done
  10.3 5.5 %collective-permute-start.3 = (f32[6,18,1,128]{3,2,1,0:T(1,128)S(1)}, f32[6,18,1,128]{3,2,1,0:T(1,128)S(1)}, u32[]{:S(2)}, u32[]{:S(2)}) collective-permute-start(f32[6,18,1,128]{3,2,1,0:T(1,128)S(1)} %get-tuple-element.49), channel_id=1, source_target_pairs={{0,1},{1,2},{2,3},{3,4},{4,5},{5,6},{6,7},{8,9},{9,10},{10,11},{11... | collective-permute-start | bytes 165896 | tf_op jit(solution)/shard_map/ppermute | solution.py:16
  15.9 1.9 collective-permute-start.2
  17.9 3.5 %collective-permute-done.2 = f32[6,18,1,128]{3,2,1,0:T(1,128)S(1)} collective-permute-done((f32[6,18,1,128]{3,2,1,0:T(1,128)S(1)}, f32[6,18,1,128]{3,2,1,0:T(1,128)S(1)}, u32[]{:S(2)}, u32[]{:S(2)}) %collective-permute-start.2) | collective-permute-done | bytes 55328 | tf_op jit(solution)/shard_map/ppermute | solution.py:19
  21.3 0.7 fusion.20
  22.2 1.2 copy-done
  23.4 1.3 collective-permute-start.4
  24.7 4.0 %collective-permute-start.5 = (f32[3,1,16,128]{3,2,1,0:T(8,128)S(1)}, f32[3,1,16,128]{3,2,1,0:T(8,128)S(1)}, u32[]{:S(2)}, u32[]{:S(2)}) collective-permute-start(f32[3,1,16,128]{3,2,1,0:T(8,128)S(1)} %get-tuple-element.72), channel_id=1, source_target_pairs={{0,8},{8,16},{16,24},{24,32},{32,40},{40,48},{48,56},{56,64},{64,7... | collective-permute-start | bytes 73736 | tf_op jit(solution)/shard_map/ppermute | solution.py:16
  28.7 0.9 collective-permute-done.5
  29.7 3.0 %collective-permute-start.7 = (f32[3,18,1,128]{3,2,1,0:T(1,128)S(1)}, f32[3,18,1,128]{3,2,1,0:T(1,128)S(1)}, u32[]{:S(2)}, u32[]{:S(2)}) collective-permute-start(f32[3,18,1,128]{3,2,1,0:T(1,128)S(1)} %get-tuple-element.65), channel_id=1, source_target_pairs={{0,1},{1,2},{2,3},{3,4},{4,5},{5,6},{6,7},{8,9},{9,10},{10,11},{11... | collective-permute-start | bytes 82952 | tf_op jit(solution)/shard_map/ppermute | solution.py:16
  32.7 1.9 collective-permute-start.6
  34.7 3.2 %collective-permute-done.6 = f32[3,18,1,128]{3,2,1,0:T(1,128)S(1)} collective-permute-done((f32[3,18,1,128]{3,2,1,0:T(1,128)S(1)}, f32[3,18,1,128]{3,2,1,0:T(1,128)S(1)}, u32[]{:S(2)}, u32[]{:S(2)}) %collective-permute-start.6) | collective-permute-done | bytes 27680 | tf_op jit(solution)/shard_map/ppermute | solution.py:19
  37.9 0.3 fusion.34
  38.3 0.3 constant_dynamic-update-slice_fusion.5
  38.7 0.7 constant_dynamic-update-slice_fusion
  39.4 3.9 %collective-permute-start.9 = (f32[6,1,16,128]{3,2,1,0:T(8,128)S(1)}, f32[6,1,16,128]{3,2,1,0:T(8,128)S(1)}, u32[]{:S(2)}, u32[]{:S(2)}) collective-permute-start(f32[6,1,16,128]{3,2,1,0:T(8,128)S(1)} %get-tuple-element.51), channel_id=1, source_target_pairs={{0,8},{8,16},{16,24},{24,32},{32,40},{40,48},{48,56},{56,64},{64,7... | collective-permute-start | bytes 147464 | tf_op jit(solution)/shard_map/ppermute | solution.py:16
  43.4 1.3 collective-permute-start.8
  44.8 3.7 %collective-permute-done.8 = f32[6,1,16,128]{3,2,1,0:T(8,128)S(1)} collective-permute-done((f32[6,1,16,128]{3,2,1,0:T(8,128)S(1)}, f32[6,1,16,128]{3,2,1,0:T(8,128)S(1)}, u32[]{:S(2)}, u32[]{:S(2)}) %collective-permute-start.8) | collective-permute-done | bytes 49184 | tf_op jit(solution)/shard_map/ppermute | solution.py:19
  48.5 3.1 %collective-permute-start.11 = (f32[6,18,1,128]{3,2,1,0:T(1,128)S(1)}, f32[6,18,1,128]{3,2,1,0:T(1,128)S(1)}, u32[]{:S(2)}, u32[]{:S(2)}) collective-permute-start(f32[6,18,1,128]{3,2,1,0:T(1,128)S(1)} %get-tuple-element.45), channel_id=1, source_target_pairs={{0,1},{1,2},{2,3},{3,4},{4,5},{5,6},{6,7},{8,9},{9,10},{10,11},{11... | collective-permute-start | bytes 165896 | tf_op jit(solution)/shard_map/ppermute | solution.py:16
  51.7 1.9 collective-permute-start.10
  53.6 0.2 fusion.41
  53.8 3.3 %collective-permute-done.10 = f32[6,18,1,128]{3,2,1,0:T(1,128)S(1)} collective-permute-done((f32[6,18,1,128]{3,2,1,0:T(1,128)S(1)}, f32[6,18,1,128]{3,2,1,0:T(1,128)S(1)}, u32[]{:S(2)}, u32[]{:S(2)}) %collective-permute-start.10) | collective-permute-done | bytes 55328 | tf_op jit(solution)/shard_map/ppermute | solution.py:19
  57.1 0.7 fusion.16
  57.8 0.1 slice_add_fusion.7
  57.9 0.1 fusion.66
  58.1 5.7 %collective-permute-start.13 = (f32[3,1,16,128]{3,2,1,0:T(8,128)S(1)}, f32[3,1,16,128]{3,2,1,0:T(8,128)S(1)}, u32[]{:S(2)}, u32[]{:S(2)}) collective-permute-start(f32[3,1,16,128]{3,2,1,0:T(8,128)S(1)} %get-tuple-element.68), channel_id=1, source_target_pairs={{0,8},{8,16},{16,24},{24,32},{32,40},{40,48},{48,56},{56,64},{64,7... | collective-permute-start | bytes 73736 | tf_op jit(solution)/shard_map/ppermute | solution.py:16
  63.8 1.3 collective-permute-start.12
  65.1 5.9 %collective-permute-done.12 = f32[3,1,16,128]{3,2,1,0:T(8,128)S(1)} collective-permute-done((f32[3,1,16,128]{3,2,1,0:T(8,128)S(1)}, f32[3,1,16,128]{3,2,1,0:T(8,128)S(1)}, u32[]{:S(2)}, u32[]{:S(2)}) %collective-permute-start.12) | collective-permute-done | bytes 24608 | tf_op jit(solution)/shard_map/ppermute | solution.py:19
  71.1 3.0 %collective-permute-start.15 = (f32[3,18,1,128]{3,2,1,0:T(1,128)S(1)}, f32[3,18,1,128]{3,2,1,0:T(1,128)S(1)}, u32[]{:S(2)}, u32[]{:S(2)}) collective-permute-start(f32[3,18,1,128]{3,2,1,0:T(1,128)S(1)} %get-tuple-element.61), channel_id=1, source_target_pairs={{0,1},{1,2},{2,3},{3,4},{4,5},{5,6},{6,7},{8,9},{9,10},{10,11},{11... | collective-permute-start | bytes 82952 | tf_op jit(solution)/shard_map/ppermute | solution.py:16
  74.1 1.9 collective-permute-start.14
  76.0 0.8 fusion.6
  76.8 0.8 all_to_all.9
  77.6 14.2 %all-to-all-start = ((f32[128,6,1]{1,2,0:T(1,128)}), f32[128,6,1]{1,2,0:T(1,128)}, u32[]{:S(2)}, u32[]{:S(2)}) async-start(f32[128,6,1]{1,2,0:T(1,128)} %bitcast.6), calls=%async_computation | async-start | bytes 131072 | tf_op jit(solution)/shard_map/all_to_all | solution.py:149
  91.8 0.2 copy.37
  92.0 0.4 fusion.32
  92.4 0.3 copy-done.1
  92.7 0.3 multiply_convert_fusion
  93.0 0.1 fusion.63
  93.1 0.1 copy.38
  93.2 0.1 copy.39
  93.3 0.1 copy.40
  93.5 0.1 copy.41
  93.6 0.1 copy.42
  93.7 0.1 copy.43
  93.9 0.8 copy-done.2
  94.6 1.6 concatenate.113
  96.2 7.0 %fusion.7 = f32[256,9,2,128]{3,1,2,0:T(8,128)S(1)} fusion(bf16[256,2,128,128]{3,2,1,0:T(8,128)(2,1)} %bitcast.56, bf16[9,256,128]{2,0,1:T(8,128)(2,1)S(1)} %concatenate.113), kind=kOutput, calls=%fused_computation.12 | convolution fusion | flops 150994944 | bytes 19726336 | tf_op jit(solution)/shard_map/cbi,boij->bocj/dot_general | solution.py:120
  103.2 2.5 %copy.50 = f32[64,8,9,128]{3,1,2,0:T(8,128)} copy(f32[64,8,9,128]{3,2,1,0:T(8,128)S(1)} %bitcast.57) | data formatting | bytes 4718592
  105.8 2.0 copy.44
  107.8 3.5 %fusion.4 = f32[768,9,128]{2,0,1:T(8,128)S(1)} fusion(f32[9,128,512]{2,1,0:T(8,128)S(1)} %bitcast.58, s32[512]{0:T(512)S(1)} %multiply_add_fusion.12), kind=kOutput, calls=%fused_computation.10 | convolution fusion | flops 5436211200 | bytes 5900288 | tf_op jit(solution)/shard_map/dot_general | solution.py:138
  111.4 4.9 %copy.45 = f32[768,9,128]{2,1,0:T(8,128)} copy(f32[768,9,128]{2,0,1:T(8,128)S(1)} %fusion.4) | data formatting | bytes 7077888 | tf_op jit(solution)/shard_map/dot_general | solution.py:138
  116.2 10.2 %all-to-all-start.1 = ((f32[768,9,128]{2,1,0:T(8,128)}), f32[768,9,128]{2,1,0:T(8,128)}, u32[]{:S(2)}, u32[]{:S(2)}) async-start(f32[768,9,128]{2,1,0:T(8,128)} %copy.45), calls=%async_computation.1 | async-start | bytes 12582912 | tf_op jit(solution)/shard_map/all_to_all | solution.py:148
  126.4 1.0 convert_reduce_fusion
  127.4 0.1 convert_element_type.34
  127.6 0.7 multiply_dynamic-update-slice_fusion
  128.3 74.7 %all-to-all-done.1 = f32[768,9,128]{2,1,0:T(8,128)} async-done(((f32[768,9,128]{2,1,0:T(8,128)}), f32[768,9,128]{2,1,0:T(8,128)}, u32[]{:S(2)}, u32[]{:S(2)}) %all-to-all-start.1) | async-done | bytes 3538976 | tf_op jit(solution)/shard_map/all_to_all | solution.py:148
  203.0 4.9 %copy.46 = f32[768,9,128]{0,2,1:T(8,128)S(1)} copy(f32[768,9,128]{2,1,0:T(8,128)} %all-to-all-done.1) | data formatting | bytes 7077888 | tf_op jit(solution)/shard_map/all_to_all | solution.py:148
  207.9 3.1 %fusion = f32[256,9,128]{2,0,1:T(8,128)} fusion(f32[768,9,128]{0,2,1:T(8,128)S(1)} %copy.46, s32[768]{0:T(1024)S(1)} %convert_element_type.34), kind=kOutput, calls=%fused_computation | convolution fusion | flops 2718105600 | bytes 4721664 | tf_op jit(solution)/shard_map/dot_general | solution.py:156
  (54 shorter events, 0.8 us)
Async XLA Ops:
  1.5 7.5 %collective-permute-start.1 = (f32[6,1,16,128]{3,2,1,0:T(8,128)S(1)}, f32[6,1,16,128]{3,2,1,0:T(8,128)S(1)}, u32[]{:S(2)}, u32[]{:S(2)}) collective-permute-start(f32[6,1,16,128]{3,2,1,0:T(8,128)S(1)} %get-tuple-element.40), channel_id=1, source_target_pairs={{0,8},{8,16},{16,24},{24,32},{32,40},{40,48},{48,56},{56,64},{64,7... | collective-permute-start | bytes 147464 | tf_op jit(solution)/shard_map/ppermute | solution.py:16
  5.4 4.8 %collective-permute-start = (f32[6,1,16,128]{3,2,1,0:T(8,128)S(1)}, f32[6,1,16,128]{3,2,1,0:T(8,128)S(1)}, u32[]{:S(2)}, u32[]{:S(2)}) collective-permute-start(f32[6,1,16,128]{3,2,1,0:T(8,128)S(1)} %get-tuple-element.41), channel_id=1, source_target_pairs={{8,0},{16,8},{24,16},{32,24},{40,32},{48,40},{56,48},{64,56},{72,6... | collective-permute-start | bytes 147464 | tf_op jit(solution)/shard_map/ppermute | solution.py:19
  7.7 10.1 %copy-start.3 = (f32[16,16,128]{2,1,0:T(8,128)S(1)}, f32[16,16,128]{2,1,0:T(8,128)}, u32[]{:S(2)}) copy-start(f32[16,16,128]{2,1,0:T(8,128)} %param.8) | copy-start | bytes 393220
  10.3 7.5 %collective-permute-start.3 = (f32[6,18,1,128]{3,2,1,0:T(1,128)S(1)}, f32[6,18,1,128]{3,2,1,0:T(1,128)S(1)}, u32[]{:S(2)}, u32[]{:S(2)}) collective-permute-start(f32[6,18,1,128]{3,2,1,0:T(1,128)S(1)} %get-tuple-element.49), channel_id=1, source_target_pairs={{0,1},{1,2},{2,3},{3,4},{4,5},{5,6},{6,7},{8,9},{9,10},{10,11},{11... | collective-permute-start | bytes 165896 | tf_op jit(solution)/shard_map/ppermute | solution.py:16
  15.9 5.5 %collective-permute-start.2 = (f32[6,18,1,128]{3,2,1,0:T(1,128)S(1)}, f32[6,18,1,128]{3,2,1,0:T(1,128)S(1)}, u32[]{:S(2)}, u32[]{:S(2)}) collective-permute-start(f32[6,18,1,128]{3,2,1,0:T(1,128)S(1)} %get-tuple-element.48), channel_id=1, source_target_pairs={{1,0},{2,1},{3,2},{4,3},{5,4},{6,5},{7,6},{9,8},{10,9},{11,10},{12... | collective-permute-start | bytes 165896 | tf_op jit(solution)/shard_map/ppermute | solution.py:19
  22.1 1.3 copy-start
  22.1 6.6 %copy-start.7 = (s32[16,16]{1,0:T(8,128)S(1)}, s32[16,16]{1,0:T(8,128)}, u32[]{:S(2)}) copy-start(s32[16,16]{1,0:T(8,128)} %param.9) | copy-start | bytes 3076
  23.4 14.9 %copy-start.4 = (f32[16,16]{1,0:T(8,128)S(1)}, f32[16,16]{1,0:T(8,128)}, u32[]{:S(2)}) copy-start(f32[16,16]{1,0:T(8,128)} %param.10) | copy-start | bytes 3076
  23.4 5.3 %collective-permute-start.4 = (f32[3,1,16,128]{3,2,1,0:T(8,128)S(1)}, f32[3,1,16,128]{3,2,1,0:T(8,128)S(1)}, u32[]{:S(2)}, u32[]{:S(2)}) collective-permute-start(f32[3,1,16,128]{3,2,1,0:T(8,128)S(1)} %get-tuple-element.71), channel_id=1, source_target_pairs={{8,0},{16,8},{24,16},{32,24},{40,32},{48,40},{56,48},{64,56},{72,6... | collective-permute-start | bytes 73736 | tf_op jit(solution)/shard_map/ppermute | solution.py:19
  24.7 4.9 %collective-permute-start.5 = (f32[3,1,16,128]{3,2,1,0:T(8,128)S(1)}, f32[3,1,16,128]{3,2,1,0:T(8,128)S(1)}, u32[]{:S(2)}, u32[]{:S(2)}) collective-permute-start(f32[3,1,16,128]{3,2,1,0:T(8,128)S(1)} %get-tuple-element.72), channel_id=1, source_target_pairs={{0,8},{8,16},{16,24},{24,32},{32,40},{40,48},{48,56},{56,64},{64,7... | collective-permute-start | bytes 73736 | tf_op jit(solution)/shard_map/ppermute | solution.py:16
  29.7 5.0 %collective-permute-start.7 = (f32[3,18,1,128]{3,2,1,0:T(1,128)S(1)}, f32[3,18,1,128]{3,2,1,0:T(1,128)S(1)}, u32[]{:S(2)}, u32[]{:S(2)}) collective-permute-start(f32[3,18,1,128]{3,2,1,0:T(1,128)S(1)} %get-tuple-element.65), channel_id=1, source_target_pairs={{0,1},{1,2},{2,3},{3,4},{4,5},{5,6},{6,7},{8,9},{9,10},{10,11},{11... | collective-permute-start | bytes 82952 | tf_op jit(solution)/shard_map/ppermute | solution.py:16
  32.7 5.2 %collective-permute-start.6 = (f32[3,18,1,128]{3,2,1,0:T(1,128)S(1)}, f32[3,18,1,128]{3,2,1,0:T(1,128)S(1)}, u32[]{:S(2)}, u32[]{:S(2)}) collective-permute-start(f32[3,18,1,128]{3,2,1,0:T(1,128)S(1)} %get-tuple-element.64), channel_id=1, source_target_pairs={{1,0},{2,1},{3,2},{4,3},{5,4},{6,5},{7,6},{9,8},{10,9},{11,10},{12... | collective-permute-start | bytes 82952 | tf_op jit(solution)/shard_map/ppermute | solution.py:19
  34.7 3.9 %copy-start.6 = (s32[128,5]{0,1:T(8,128)}, s32[128,5]{0,1:T(8,128)S(1)}, u32[]{:S(2)}) copy-start(s32[128,5]{0,1:T(8,128)S(1)} %reduce-window.9) | copy-start | bytes 7684
  38.6 6.1 %slice-start = ((s32[128,5]{0,1:T(8,128)}), s32[128,4]{0,1:T(4,128)S(1)}, s32[]{:S(2)}) async-start(s32[128,5]{0,1:T(8,128)} %copy-done.6), calls=%async_computation.2 | async-start | bytes 4096 | tf_op jit(solution)/shard_map/slice.1
  39.4 14.2 %copy-start.5 = (s32[512,1]{0,1:T(1,128)S(1)}, s32[512,1]{0,1:T(1,128)}, u32[]{:S(2)}) copy-start(s32[512,1]{0,1:T(1,128)} %param.12) | copy-start | bytes 6148
  39.4 5.3 %collective-permute-start.9 = (f32[6,1,16,128]{3,2,1,0:T(8,128)S(1)}, f32[6,1,16,128]{3,2,1,0:T(8,128)S(1)}, u32[]{:S(2)}, u32[]{:S(2)}) collective-permute-start(f32[6,1,16,128]{3,2,1,0:T(8,128)S(1)} %get-tuple-element.51), channel_id=1, source_target_pairs={{0,8},{8,16},{16,24},{24,32},{32,40},{40,48},{48,56},{56,64},{64,7... | collective-permute-start | bytes 147464 | tf_op jit(solution)/shard_map/ppermute | solution.py:16
  43.4 5.1 %collective-permute-start.8 = (f32[6,1,16,128]{3,2,1,0:T(8,128)S(1)}, f32[6,1,16,128]{3,2,1,0:T(8,128)S(1)}, u32[]{:S(2)}, u32[]{:S(2)}) collective-permute-start(f32[6,1,16,128]{3,2,1,0:T(8,128)S(1)} %get-tuple-element.52), channel_id=1, source_target_pairs={{8,0},{16,8},{24,16},{32,24},{40,32},{48,40},{56,48},{64,56},{72,6... | collective-permute-start | bytes 147464 | tf_op jit(solution)/shard_map/ppermute | solution.py:19
  48.5 5.3 %collective-permute-start.11 = (f32[6,18,1,128]{3,2,1,0:T(1,128)S(1)}, f32[6,18,1,128]{3,2,1,0:T(1,128)S(1)}, u32[]{:S(2)}, u32[]{:S(2)}) collective-permute-start(f32[6,18,1,128]{3,2,1,0:T(1,128)S(1)} %get-tuple-element.45), channel_id=1, source_target_pairs={{0,1},{1,2},{2,3},{3,4},{4,5},{5,6},{6,7},{8,9},{9,10},{10,11},{11... | collective-permute-start | bytes 165896 | tf_op jit(solution)/shard_map/ppermute | solution.py:16
  51.7 5.5 %collective-permute-start.10 = (f32[6,18,1,128]{3,2,1,0:T(1,128)S(1)}, f32[6,18,1,128]{3,2,1,0:T(1,128)S(1)}, u32[]{:S(2)}, u32[]{:S(2)}) collective-permute-start(f32[6,18,1,128]{3,2,1,0:T(1,128)S(1)} %get-tuple-element.44), channel_id=1, source_target_pairs={{1,0},{2,1},{3,2},{4,3},{5,4},{6,5},{7,6},{9,8},{10,9},{11,10},{12... | collective-permute-start | bytes 165896 | tf_op jit(solution)/shard_map/ppermute | solution.py:19
  57.9 7.2 %copy-start.8 = (s32[512]{0:T(512)S(1)}, s32[512]{0:T(512)}, u32[]{:S(2)}) copy-start(s32[512]{0:T(512)} %param.13) | copy-start | bytes 6148
  58.1 7.1 %collective-permute-start.13 = (f32[3,1,16,128]{3,2,1,0:T(8,128)S(1)}, f32[3,1,16,128]{3,2,1,0:T(8,128)S(1)}, u32[]{:S(2)}, u32[]{:S(2)}) collective-permute-start(f32[3,1,16,128]{3,2,1,0:T(8,128)S(1)} %get-tuple-element.68), channel_id=1, source_target_pairs={{0,8},{8,16},{16,24},{24,32},{32,40},{40,48},{48,56},{56,64},{64,7... | collective-permute-start | bytes 73736 | tf_op jit(solution)/shard_map/ppermute | solution.py:16
  63.8 7.3 %collective-permute-start.12 = (f32[3,1,16,128]{3,2,1,0:T(8,128)S(1)}, f32[3,1,16,128]{3,2,1,0:T(8,128)S(1)}, u32[]{:S(2)}, u32[]{:S(2)}) collective-permute-start(f32[3,1,16,128]{3,2,1,0:T(8,128)S(1)} %get-tuple-element.69), channel_id=1, source_target_pairs={{8,0},{16,8},{24,16},{32,24},{40,32},{48,40},{56,48},{64,56},{72,6... | collective-permute-start | bytes 73736 | tf_op jit(solution)/shard_map/ppermute | solution.py:19
  71.1 20.9 %collective-permute-start.15 = (f32[3,18,1,128]{3,2,1,0:T(1,128)S(1)}, f32[3,18,1,128]{3,2,1,0:T(1,128)S(1)}, u32[]{:S(2)}, u32[]{:S(2)}) collective-permute-start(f32[3,18,1,128]{3,2,1,0:T(1,128)S(1)} %get-tuple-element.61), channel_id=1, source_target_pairs={{0,1},{1,2},{2,3},{3,4},{4,5},{5,6},{6,7},{8,9},{9,10},{10,11},{11... | collective-permute-start | bytes 82952 | tf_op jit(solution)/shard_map/ppermute | solution.py:16
  74.1 17.9 %collective-permute-start.14 = (f32[3,18,1,128]{3,2,1,0:T(1,128)S(1)}, f32[3,18,1,128]{3,2,1,0:T(1,128)S(1)}, u32[]{:S(2)}, u32[]{:S(2)}) collective-permute-start(f32[3,18,1,128]{3,2,1,0:T(1,128)S(1)} %get-tuple-element.60), channel_id=1, source_target_pairs={{1,0},{2,1},{3,2},{4,3},{5,4},{6,5},{7,6},{9,8},{10,9},{11,10},{12... | collective-permute-start | bytes 82952 | tf_op jit(solution)/shard_map/ppermute | solution.py:19
  77.6 38.6 %all-to-all-start = ((f32[128,6,1]{1,2,0:T(1,128)}), f32[128,6,1]{1,2,0:T(1,128)}, u32[]{:S(2)}, u32[]{:S(2)}) async-start(f32[128,6,1]{1,2,0:T(1,128)} %bitcast.6), calls=%async_computation | async-start | bytes 131072 | tf_op jit(solution)/shard_map/all_to_all | solution.py:149
  91.8 0.9 copy-start.1
  93.6 1.0 copy-start.2
  116.2 86.8 %all-to-all-start.1 = ((f32[768,9,128]{2,1,0:T(8,128)}), f32[768,9,128]{2,1,0:T(8,128)}, u32[]{:S(2)}, u32[]{:S(2)}) async-start(f32[768,9,128]{2,1,0:T(8,128)} %copy.45), calls=%async_computation.1 | async-start | bytes 12582912 | tf_op jit(solution)/shard_map/all_to_all | solution.py:148
where the time goes:
time: 212 us; the launch traced here: 211 us
  waiting for transfers between devices  96.5 us (46%)
  starting transfers between devices  69.5 us (33%)
  local copies, waits for them, and re-layouts  22.8 us (11%)
  matrix products  14.4 us (7%)
  other arithmetic  6.44 us (3%)
    all_to_all x1, waiting for transfers between devices, on_device(): lax.all_to_all(outgoing, ('cut', 'depth'), split_axis=0, concat_axis=0, t...  74.7 us
    ppermute x8, starting transfers between devices, with_halo(): lax.ppermute(lax.slice_in_dim(block, block.shape[dim] - width, None, axis...  32.3 us
    ppermute x8, waiting for transfers between devices, with_halo(): lax.ppermute(lax.slice_in_dim(block, 0, width, axis=dim), axis, backward)  20.9 us
    all_to_all x1, starting transfers between devices, on_device(): lax.all_to_all(labels, ('cut', 'depth'), split_axis=0, concat_axis=0, til...  14.2 us
    ppermute x8, starting transfers between devices, with_halo(): lax.ppermute(lax.slice_in_dim(block, 0, width, axis=dim), axis, backward)  12.9 us
    all_to_all x1, starting transfers between devices, on_device(): lax.all_to_all(outgoing, ('cut', 'depth'), split_axis=0, concat_axis=0, t...  10.2 us
    dot_general x1, matrix products, on_device(): jnp.einsum('cbi,boij->bocj', fields, weight_blocks, preferred_element_typ...  7.02 us
    dot_general x2, local copies, waits for them, and re-layouts, on_device(): jnp.dot(placing, contribution, precision=lax.Precision.HIGHEST, preferred...  6.89 us
  transfers between devices with their start and end apart: 18, of which 8 were waited for; matrix products, arithmetic and copies ran while one was open for 13% of the time, Pallas kernels for 0%

commit v1 on v0

v1 whole, which is shorter than its diff:
```python
import jax
import jax.numpy as jnp
from jax import lax
from jax.experimental import pallas as pl
from jax.experimental.pallas import tpu as pltpu
from jax.sharding import PartitionSpec as P

f32 = jnp.float32
N = 16
R = 4
E = N + 2 * R
W = 128
DEV = 128
CAP = 6
TILES = CAP + 1
SLABS = 6 * 4 + 3 * 3 + 3 + 2
INNER = 22
DEP = INNER * 4
DEPTH_ROWS = 10 * DEP + 40
SLOTS = 256
VMEM_LIMIT = 52 * 1024 * 1024
BIG = 1e30


def slab_of(field, offset):
    if field < 6:
        return field * 4 + offset
    if field < 9:
        return 24 + (field - 6) * 3 + offset
    if field == 9:
        return 33 + offset
    return 36 + offset


def reach_of(field):
    return 4 if field < 6 else (3 if field < 10 else 2)


def own_row(field, row, state_ref, inv, limit_ref):
    if field < 6:
        return state_ref[3 + field, row]
    if field < 9:
        return state_ref[field - 6, row]
    if field == 9:
        return inv(row)
    return limit_ref[row]


def pack_cut(state_ref, density_ref, limit_ref, low_ref, high_ref):
    def inv(row):
        return 0.075 / density_ref[row]

    for field in range(11):
        reach = reach_of(field)
        for offset in range(reach):
            low_ref[slab_of(field, offset)] = own_row(field, offset, state_ref, inv, limit_ref)
            high_ref[slab_of(field, offset)] = own_row(
                field, N - reach + offset, state_ref, inv, limit_ref
            )


def extended_row(field, r, state_ref, inv, limit_ref, from_low_ref, from_high_ref):
    if r < R:
        return from_low_ref[slab_of(field, r - (R - reach_of(field)))]
    if r >= R + N:
        return from_high_ref[slab_of(field, r - R - N)]
    return own_row(field, r - R, state_ref, inv, limit_ref)


def pack_depth(state_ref, density_ref, limit_ref, from_low_ref, from_high_ref, low_ref, high_ref):
    def inv(row):
        return 0.075 / density_ref[row]

    for field in range(10):
        for r in range(1, 1 + INNER):
            row = extended_row(field, r, state_ref, inv, limit_ref, from_low_ref, from_high_ref)
            at = field * DEP + (r - 1) * 4
            low_ref[at : at + 4] = row[:4]
            high_ref[at : at + 4] = row[12:]
    for r in range(3, 21):
        row = extended_row(10, r, state_ref, inv, limit_ref, from_low_ref, from_high_ref)
        at = 10 * DEP + (r - 3) * 2
        low_ref[at : at + 2] = row[:2]
        high_ref[at : at + 2] = row[14:]


def steps_and_remap(
    place_ref,
    state_ref,
    density_ref,
    limit_ref,
    cut_low_ref,
    cut_high_ref,
    depth_low_ref,
    depth_high_ref,
    labels_ref,
    weights_ref,
    after_ref,
    outgoing_ref,
    ext,
    rows,
    held,
    sems,
):
    per = 2 * N

    def fetch(cx):
        return pltpu.make_async_copy(
            weights_ref.at[pl.ds(cx * per, per)], held.at[pl.ds(cx * per, per)], sems.at[cx]
        )

    for cx in range(N):
        fetch(cx).start()

    def inv(row):
        return 0.075 / density_ref[row]

    zeros4 = jnp.zeros((4, W), f32)
    zeros2 = jnp.zeros((2, W), f32)
    for field in range(11):
        reach = reach_of(field)
        for r in range(R - reach, R + N + reach):
            row = extended_row(field, r, state_ref, inv, limit_ref, cut_low_ref, cut_high_ref)
            if field < 10 and 1 <= r <= INNER:
                at = field * DEP + (r - 1) * 4
                low, high = depth_low_ref[at : at + 4], depth_high_ref[at : at + 4]
            elif field == 10 and 3 <= r <= 20:
                at = 10 * DEP + (r - 3) * 2
                low = jnp.concatenate([zeros2, depth_low_ref[at : at + 2]], 0)
                high = jnp.concatenate([depth_high_ref[at : at + 2], zeros2], 0)
            else:
                low = high = zeros4
            ext[field, r] = jnp.concatenate([low, row, high], 0)

    def label(owner, carry):
        outgoing_ref[owner * TILES + CAP] = jnp.broadcast_to(labels_ref[owner], (8, W))
        return carry

    lax.fori_loop(0, DEV, label, 0)

    lane = lax.broadcasted_iota(jnp.int32, (E, W), 1)
    first, last = lane == 0, lane == W - 1

    def along_depth(x):
        return pltpu.roll(x, E - 1, 0) - pltpu.roll(x, 1, 0)

    def along_width(x):
        up = jnp.where(last, 0.0, pltpu.roll(x, W - 1, 1))
        down = jnp.where(first, 0.0, pltpu.roll(x, 1, 1))
        return up - down

    def velocity(r, carry):
        def along_cut(field):
            return ext[field, r + 1] - ext[field, r - 1]

        scale = ext[9, r]
        xy, yz, xz = ext[3, r], ext[4, r], ext[5, r]
        ext[6, r] += (along_cut(0) + along_depth(xy) + along_width(xz)) * scale
        ext[7, r] += (along_cut(3) + along_depth(ext[1, r]) + along_width(yz)) * scale
        ext[8, r] += (along_cut(5) + along_depth(yz) + along_width(ext[2, r])) * scale
        return carry

    def stress(r):
        vx, vy, vz = ext[6, r], ext[7, r], ext[8, r]
        limit = ext[10, r]

        def along_cut(field):
            return ext[field, r + 1] - ext[field, r - 1]

        xx, yy, zz = along_cut(6), along_depth(vy), along_width(vz)
        bulk = 0.075 * (xx + yy + zz)
        sxx = ext[0, r] + (0.09 * xx + bulk)
        syy = ext[1, r] + (0.09 * yy + bulk)
        szz = ext[2, r] + (0.09 * zz + bulk)
        sxy = ext[3, r] + 0.045 * (along_depth(vx) + along_cut(7))
        syz = ext[4, r] + 0.045 * (along_width(vy) + along_depth(vz))
        sxz = ext[5, r] + 0.045 * (along_width(vx) + along_cut(8))
        p = (sxx + syy + szz) * (1.0 / 3.0)
        dxx, dyy, dzz = sxx - p, syy - p, szz - p
        square = 1.5 * (
            dxx * dxx + dyy * dyy + dzz * dzz + 2.0 * (sxy * sxy + syz * syz + sxz * sxz)
        )
        factor = jnp.minimum(1.0, limit * lax.rsqrt(square))
        inside = limit > 0.0
        new = (
            p + factor * dxx,
            p + factor * dyy,
            p + factor * dzz,
            factor * sxy,
            factor * syz,
            factor * sxz,
        )
        return [jnp.where(inside, x, 0.0) for x in new]

    def stress_loop(r, carry):
        for field, x in enumerate(stress(r)):
            ext[field, r] = x
        return carry

    lax.fori_loop(1, 23, velocity, 0)
    lax.fori_loop(2, 22, stress_loop, 0)
    lax.fori_loop(3, 21, velocity, 0)

    def remap(cx, carry):
        r = cx + R
        fields = [ext[6, r], ext[7, r], ext[8, r]] + stress(r)
        for field, x in enumerate(fields):
            own = x[R : R + N]
            after_ref[field, cx] = own
            rows[pl.ds(field, N, stride=16)] = own
        fetch(cx).wait()
        for cy in range(N):
            block = rows[cy * 16 : (cy + 1) * 16].astype(jnp.bfloat16)
            for crossing in range(2):
                pair = cx * per + 2 * cy + crossing
                result = jnp.dot(block, held[pair], preferred_element_type=f32)
                place = place_ref[pair]
                base = (place >> 3) * TILES
                rank = place & 7
                outgoing_ref[base + rank] = result[:8]
                outgoing_ref[base + CAP, pl.ds(rank, 1)] = result[8:9]
        return carry

    lax.fori_loop(0, N, remap, 0)


PARTS = 3
ROOM = SLOTS + 8


def gather(slots_ref, arrived_ref, out_ref, *sums):
    main, rest = sums[:PARTS], sums[PARTS:]
    for k in range(PARTS):
        main[k][...] = jnp.zeros((8 * ROOM, W), f32)
        rest[k][...] = jnp.zeros((ROOM, W), f32)

    def add(source, carry):
        for k in range(CAP):
            slot = slots_ref[source * CAP + k]
            part = k % PARTS
            tile = pl.ds(pl.multiple_of(slot * 8, 8), 8)
            main[part][tile] += arrived_ref[source * TILES + k]
            rest[part][pl.ds(slot, 1)] += arrived_ref[source * TILES + CAP, k : k + 1]
        return carry

    lax.fori_loop(0, DEV, add, 0)
    for field in range(8):
        spot = pl.ds(field, SLOTS, stride=8)
        out_ref[field] = main[0][spot] + main[1][spot] + main[2][spot]
    out_ref[8] = rest[0][:SLOTS] + rest[1][:SLOTS] + rest[2][:SLOTS]


def exchange(low, high, axis):
    count = lax.axis_size(axis)
    up = [(i, i + 1) for i in range(count - 1)]
    down = [(target, source) for source, target in up]
    return lax.ppermute(high, axis, up), lax.ppermute(low, axis, down)


VM = pl.BlockSpec(memory_space=pltpu.VMEM)
SM = pl.BlockSpec(memory_space=pltpu.SMEM)
HB = pl.BlockSpec(memory_space=pl.ANY)
PARAMS = pltpu.CompilerParams(vmem_limit_bytes=VMEM_LIMIT)


def on_device(
    initial_state, density, yield_flags, yield_stress, crossing_weights, new_owner, new_slot
):
    limit = jnp.broadcast_to(
        jnp.where(yield_flags == 1, yield_stress, BIG)[:, :, None], (N, N, W)
    )
    cut_shape = jax.ShapeDtypeStruct((SLABS, N, W), f32)
    low, high = pl.pallas_call(
        pack_cut,
        out_shape=(cut_shape, cut_shape),
        in_specs=[VM] * 3,
        out_specs=(VM, VM),
        compiler_params=PARAMS,
        name="pack_cut",
    )(initial_state, density, limit)
    cut_low, cut_high = exchange(low, high, "cut")
    depth_shape = jax.ShapeDtypeStruct((DEPTH_ROWS, W), f32)
    low, high = pl.pallas_call(
        pack_depth,
        out_shape=(depth_shape, depth_shape),
        in_specs=[VM] * 5,
        out_specs=(VM, VM),
        compiler_params=PARAMS,
        name="pack_depth",
    )(initial_state, density, limit, cut_low, cut_high)
    depth_low, depth_high = exchange(low, high, "depth")

    owners = new_owner[:, 0]
    hits = (owners[:, None] == jnp.arange(DEV, dtype=jnp.int32)[None, :]).astype(jnp.int32)
    rank = jnp.sum((jnp.cumsum(hits, 0) - hits) * hits, 1)
    place = owners * 8 + rank
    by_rank = jnp.where(
        rank[:, None] == jnp.arange(W, dtype=jnp.int32)[None, :], new_slot[:, None] + 1, 0
    )
    labels = lax.dot_general(
        hits.astype(jnp.bfloat16),
        by_rank.astype(jnp.bfloat16),
        (((0,), (0,)), ((), ())),
        preferred_element_type=f32,
    )

    state_after, outgoing = pl.pallas_call(
        steps_and_remap,
        out_shape=(
            jax.ShapeDtypeStruct((9, N, N, W), f32),
            jax.ShapeDtypeStruct((DEV * TILES, 8, W), f32),
        ),
        in_specs=[SM] + [VM] * 8 + [HB],
        out_specs=(VM, VM),
        scratch_shapes=[
            pltpu.VMEM((11, E, E, W), f32),
            pltpu.VMEM((N * 16, W), f32),
            pltpu.VMEM((2 * N * N, W, W), jnp.bfloat16),
            pltpu.SemaphoreType.DMA((N,)),
        ],
        compiler_params=PARAMS,
        name="steps_and_remap",
    )(
        place,
        initial_state,
        density,
        limit,
        cut_low,
        cut_high,
        depth_low,
        depth_high,
        labels[:, None, :],
        crossing_weights,
    )
    arrived = lax.all_to_all(outgoing, ("cut", "depth"), split_axis=0, concat_axis=0, tiled=True)
    slots = arrived.reshape(DEV, TILES, 8, W)[:, CAP, CAP, :CAP].astype(jnp.int32).reshape(-1)
    slots = jnp.where(slots == 0, SLOTS, slots - 1)
    new_integrals = pl.pallas_call(
        gather,
        out_shape=jax.ShapeDtypeStruct((9, SLOTS, W), f32),
        in_specs=[SM, VM],
        out_specs=VM,
        scratch_shapes=[pltpu.VMEM((8 * ROOM, W), f32)] * PARTS
        + [pltpu.VMEM((ROOM, W), f32)] * PARTS,
        compiler_params=PARAMS,
        name="gather",
    )(slots, arrived)
    return (state_after, new_integrals.transpose(1, 0, 2))


def solution(mesh):
    return jax.shard_map(
        on_device,
        mesh=mesh,
        in_specs=(
            P(None, "cut", "depth", None),
            P("cut", "depth", None),
            P("cut", "depth"),
            P("cut", "depth"),
            P(("cut", "depth"), None, None),
            P(("cut", "depth"), None),
            P(("cut", "depth")),
        ),
        out_specs=(P(None, "cut", "depth", None), P(("cut", "depth"), None, None)),
        check_vma=False,
    )
```

time: 212 us -> 121 us (0.57)
  waiting for transfers between devices: 96.5 us -> 14 us
  blocking collectives: 0 us -> 58.3 us
  starting transfers between devices: 69.5 us -> 12.5 us
  Pallas kernels: 0 us -> 27.7 us
  local copies, waits for them, and re-layouts: 22.8 us -> 4.64 us
  matrix products: 14.4 us -> 0.44 us
  other arithmetic: 6.44 us -> 1.92 us
    all_to_all x2 -> x0, waiting for transfers between devices: 74.7 us -> none  [the longest x1 74.7 us: on_device(): lax.all_to_all(outgoing, ('cut', 'depth'), split_axis=0, concat_axis=0, t...]
    all_to_all x0 -> x1, blocking collectives: none -> 58.3 us  [on_device(): lax.all_to_all(outgoing, ('cut', 'depth'), split_axis=0, concat_axis=0, t...]
    ppermute x16 -> x4, starting transfers between devices: 45.1 us -> 12.5 us  [exchange(): return (lax.ppermute(high, axis, up), lax.ppermute(low, axis, down))]
    pallas_call x0 -> x4, Pallas kernels: none -> 27.7 us  [the longest x1 19 us: on_device(): pl.pallas_call(steps_and_remap, out_shape=(jax.ShapeDtypeStruct((9, N, N,...]
    all_to_all x2 -> x0, starting transfers between devices: 24.4 us -> none  [the longest x1 14.2 us: on_device(): lax.all_to_all(labels, ('cut', 'depth'), split_axis=0, concat_axis=0, til...]
    dot_general x4 -> x1, matrix products: 14.4 us -> 0.44 us  [on_device(): lax.dot_general(hits.astype(jnp.bfloat16), by_rank.astype(jnp.bfloat16),...]
    ppermute x16 -> x4, waiting for transfers between devices: 21.8 us -> 14 us  [exchange(): return (lax.ppermute(high, axis, up), lax.ppermute(low, axis, down))]
    dot_general x2 -> x0, local copies, waits for them, and re-layouts: 6.89 us -> none  [on_device(): jnp.dot(placing, contribution, precision=lax.Precision.HIGHEST, preferred...]
  transfers between devices with their start and end apart: 18 -> 4, of which waited for: 8 -> 4; matrix products, arithmetic and copies ran while one was open for 13% -> 2% of each run, Pallas kernels for 0% -> 0%
where the time goes in v1:
time: 121 us; the launch traced here: 120 us
  blocking collectives  58.3 us (48%)
  Pallas kernels  27.7 us (23%)
  waiting for transfers between devices  14 us (12%)
  starting transfers between devices  12.5 us (10%)
  local copies, waits for them, and re-layouts  4.64 us (4%)
  other arithmetic  1.92 us (2%)
    all_to_all x1, blocking collectives, on_device(): lax.all_to_all(outgoing, ('cut', 'depth'), split_axis=0, concat_axis=0, t...  58.3 us
    pallas_call x1, Pallas kernels, on_device(): pl.pallas_call(steps_and_remap, out_shape=(jax.ShapeDtypeStruct((9, N, N,...  19 us
    ppermute x4, waiting for transfers between devices, exchange(): return (lax.ppermute(high, axis, up), lax.ppermute(low, axis, down))  14 us
    ppermute x4, starting transfers between devices, exchange(): return (lax.ppermute(high, axis, up), lax.ppermute(low, axis, down))  12.5 us
    pallas_call x1, Pallas kernels, on_device(): pl.pallas_call(gather, out_shape=jax.ShapeDtypeStruct((9, SLOTS, W), f32)...  5.91 us
    unnamed x9, local copies, waits for them, and re-layouts  3.55 us
  transfers between devices with their start and end apart: 4, of which 4 were waited for; matrix products, arithmetic and copies ran while one was open for 2% of the time, Pallas kernels for 0%

profile of v1, /device:TPU:1, one launch (start us, length us, event | category | flops | bytes accessed | tf_op | source)
XLA Modules:
  0.0 120.2 jit_solution(9956963357329700339)
XLA Ops:
  0.6 0.0 copy-start.3
  0.6 0.7 compare_select_fusion
  1.4 0.1 broadcast_in_dim.32.limit_ref
  1.5 0.0 copy-start
  1.5 0.9 copy-done
  2.4 1.3 %pack_cut.1 = (f32[38,16,128]{2,1,0:T(8,128)S(1)}, f32[38,16,128]{2,1,0:T(8,128)S(1)}) custom-call(f32[9,16,16,128]{3,2,1,0:T(8,128)} %state_ref.5, f32[16,16,128]{2,1,0:T(8,128)S(1)} %copy-done, f32[16,16,128]{2,1,0:T(8,128)S(1)} %broadcast_in_dim.32.limit_ref), custom_call_target="tpu_custom_call" | custom-call | tf_op jit(solution)/shard_map/pack_cut/pallas_call | solution.py:273
  3.7 4.0 %collective-permute-start = (f32[38,16,128]{2,1,0:T(8,128)S(1)}, f32[38,16,128]{2,1,0:T(8,128)S(1)}, u32[]{:S(2)}, u32[]{:S(2)}) collective-permute-start(f32[38,16,128]{2,1,0:T(8,128)S(1)} %get-tuple-element.8), channel_id=1, source_target_pairs={{0,8},{8,16},{16,24},{24,32},{32,40},{40,48},{48,56},{56,64},{64,7... | collective-permute-start | bytes 933896 | tf_op jit(solution)/shard_map/ppermute | solution.py:257
  7.7 1.3 %collective-permute-start.1 = (f32[38,16,128]{2,1,0:T(8,128)S(1)}, f32[38,16,128]{2,1,0:T(8,128)S(1)}, u32[]{:S(2)}, u32[]{:S(2)}) collective-permute-start(f32[38,16,128]{2,1,0:T(8,128)S(1)} %get-tuple-element.9), channel_id=1, source_target_pairs={{8,0},{16,8},{24,16},{32,24},{40,32},{48,40},{56,48},{64,56},{72,6... | collective-permute-start | bytes 933896 | tf_op jit(solution)/shard_map/ppermute | solution.py:257
  9.0 0.8 copy.10
  9.8 0.2 fusion.2
  10.1 0.7 broadcast_add_fusion.1
  10.8 2.9 %collective-permute-done.from_low_ref.cut_low_ref = f32[38,16,128]{2,1,0:T(8,128)S(1)} collective-permute-done((f32[38,16,128]{2,1,0:T(8,128)S(1)}, f32[38,16,128]{2,1,0:T(8,128)S(1)}, u32[]{:S(2)}, u32[]{:S(2)}) %collective-permute-start) | collective-permute-done | bytes 311328 | tf_op jit(solution)/shard_map/ppermute | solution.py:257
  13.7 3.8 %collective-permute-done.1.from_high_ref.cut_high_ref = f32[38,16,128]{2,1,0:T(8,128)S(1)} collective-permute-done((f32[38,16,128]{2,1,0:T(8,128)S(1)}, f32[38,16,128]{2,1,0:T(8,128)S(1)}, u32[]{:S(2)}, u32[]{:S(2)}) %collective-permute-start.1) | collective-permute-done | bytes 311328 | tf_op jit(solution)/shard_map/ppermute | solution.py:257
  17.5 0.0 copy-start.1
  17.5 0.9 copy-done.1
  18.4 1.4 %pack_depth.1 = (f32[920,128]{1,0:T(8,128)S(1)}, f32[920,128]{1,0:T(8,128)S(1)}) custom-call(f32[9,16,16,128]{3,2,1,0:T(8,128)} %state_ref.5, f32[16,16,128]{2,1,0:T(8,128)S(1)} %copy-done.1, f32[16,16,128]{2,1,0:T(8,128)S(1)} %broadcast_in_dim.32.limit_ref, f32[38,16,128]{2,1,0:T(8,128)S(1)} %collective-permute-done.from_low_ref.cut_low_ref, ...), custom_call_target="tpu_custom_call" | custom-call | tf_op jit(solution)/shard_map/pack_depth/pallas_call | solution.py:283
  19.8 5.3 %collective-permute-start.2 = (f32[920,128]{1,0:T(8,128)S(1)}, f32[920,128]{1,0:T(8,128)S(1)}, u32[]{:S(2)}, u32[]{:S(2)}) collective-permute-start(f32[920,128]{1,0:T(8,128)S(1)} %get-tuple-element.10), channel_id=1, source_target_pairs={{0,1},{1,2},{2,3},{3,4},{4,5},{5,6},{6,7},{8,9},{9,10},{10,11},{11... | collective-permute-start | bytes 1413128 | tf_op jit(solution)/shard_map/ppermute | solution.py:257
  25.1 1.9 %collective-permute-start.3 = (f32[920,128]{1,0:T(8,128)S(1)}, f32[920,128]{1,0:T(8,128)S(1)}, u32[]{:S(2)}, u32[]{:S(2)}) collective-permute-start(f32[920,128]{1,0:T(8,128)S(1)} %get-tuple-element.11), channel_id=1, source_target_pairs={{1,0},{2,1},{3,2},{4,3},{5,4},{6,5},{7,6},{9,8},{10,9},{11,10},{12... | collective-permute-start | bytes 1413128 | tf_op jit(solution)/shard_map/ppermute | solution.py:257
  27.0 0.0 copy-done.3
  27.0 0.2 fusion.1
  27.3 0.4 fusion.4
  27.7 2.9 %collective-permute-done.2.depth_low_ref = f32[920,128]{1,0:T(8,128)S(1)} collective-permute-done((f32[920,128]{1,0:T(8,128)S(1)}, f32[920,128]{1,0:T(8,128)S(1)}, u32[]{:S(2)}, u32[]{:S(2)}) %collective-permute-start.2) | collective-permute-done | bytes 471072 | tf_op jit(solution)/shard_map/ppermute | solution.py:257
  30.6 4.4 %collective-permute-done.3.depth_high_ref = f32[920,128]{1,0:T(8,128)S(1)} collective-permute-done((f32[920,128]{1,0:T(8,128)S(1)}, f32[920,128]{1,0:T(8,128)S(1)}, u32[]{:S(2)}, u32[]{:S(2)}) %collective-permute-start.3) | collective-permute-done | bytes 471072 | tf_op jit(solution)/shard_map/ppermute | solution.py:257
  35.0 19.0 %steps_and_remap.1 = (f32[9,16,16,128]{3,2,1,0:T(8,128)}, f32[896,8,128]{2,1,0:T(8,128)}) custom-call(s32[512]{0:T(512)S(1)} %multiply_add_fusion.place_ref, f32[9,16,16,128]{3,2,1,0:T(8,128)} %state_ref.5, f32[16,16,128]{2,1,0:T(8,128)S(1)} %copy-done.1, f32[16,16,128]{2,1,0:T(8,128)S(1)} %broadcast_in_dim.32.limit_ref, ...), custom_call_target="tpu_custom_call" | custom-call | tf_op jit(solution)/shard_map/steps_and_remap/pallas_call | solution.py:307
  54.0 58.3 %all_to_all.5.arrived_ref = f32[896,8,128]{2,1,0:T(8,128)S(1)} all-to-all(f32[896,8,128]{2,1,0:T(8,128)} %get-tuple-element.13), channel_id=1, replica_groups=mesh['cut'=16,'depth'=8] {'cut','depth'}, dimensions={0} | all-to-all | bytes 7340032 | tf_op jit(solution)/shard_map/all_to_all | solution.py:335
  112.3 0.0 copy-start.2
  112.3 0.1 slice.13
  112.4 1.7 %copy-done.2 = f32[896,8,128]{2,1,0:T(8,128)} copy-done((f32[896,8,128]{2,1,0:T(8,128)}, f32[896,8,128]{2,1,0:T(8,128)S(1)}, u32[]{:S(2)}) %copy-start.2) | copy-done | bytes 3670040
  114.1 0.1 select_n.17.slots_ref
  114.2 5.9 %gather.1 = f32[9,256,128]{2,1,0:T(8,128)} custom-call(s32[768]{0:T(1024)S(1)} %select_n.17.slots_ref, f32[896,8,128]{2,1,0:T(8,128)} %copy-done.2), custom_call_target="tpu_custom_call" | custom-call | tf_op jit(solution)/shard_map/gather/pallas_call | solution.py:338
  (8 shorter events, 0.1 us)
Async XLA Ops:
  0.6 26.4 %copy-start.3 = (s32[512,1]{0,1:T(1,128)S(1)}, s32[512,1]{0,1:T(1,128)}, u32[]{:S(2)}) copy-start(s32[512,1]{0,1:T(1,128)} %param.12) | copy-start | bytes 6148
  1.5 0.9 copy-start
  3.7 10.0 %collective-permute-start = (f32[38,16,128]{2,1,0:T(8,128)S(1)}, f32[38,16,128]{2,1,0:T(8,128)S(1)}, u32[]{:S(2)}, u32[]{:S(2)}) collective-permute-start(f32[38,16,128]{2,1,0:T(8,128)S(1)} %get-tuple-element.8), channel_id=1, source_target_pairs={{0,8},{8,16},{16,24},{24,32},{32,40},{40,48},{48,56},{56,64},{64,7... | collective-permute-start | bytes 933896 | tf_op jit(solution)/shard_map/ppermute | solution.py:257
  7.7 9.8 %collective-permute-start.1 = (f32[38,16,128]{2,1,0:T(8,128)S(1)}, f32[38,16,128]{2,1,0:T(8,128)S(1)}, u32[]{:S(2)}, u32[]{:S(2)}) collective-permute-start(f32[38,16,128]{2,1,0:T(8,128)S(1)} %get-tuple-element.9), channel_id=1, source_target_pairs={{8,0},{16,8},{24,16},{32,24},{40,32},{48,40},{56,48},{64,56},{72,6... | collective-permute-start | bytes 933896 | tf_op jit(solution)/shard_map/ppermute | solution.py:257
  17.5 0.9 copy-start.1
  19.8 10.8 %collective-permute-start.2 = (f32[920,128]{1,0:T(8,128)S(1)}, f32[920,128]{1,0:T(8,128)S(1)}, u32[]{:S(2)}, u32[]{:S(2)}) collective-permute-start(f32[920,128]{1,0:T(8,128)S(1)} %get-tuple-element.10), channel_id=1, source_target_pairs={{0,1},{1,2},{2,3},{3,4},{4,5},{5,6},{6,7},{8,9},{9,10},{10,11},{11... | collective-permute-start | bytes 1413128 | tf_op jit(solution)/shard_map/ppermute | solution.py:257
  25.1 9.9 %collective-permute-start.3 = (f32[920,128]{1,0:T(8,128)S(1)}, f32[920,128]{1,0:T(8,128)S(1)}, u32[]{:S(2)}, u32[]{:S(2)}) collective-permute-start(f32[920,128]{1,0:T(8,128)S(1)} %get-tuple-element.11), channel_id=1, source_target_pairs={{1,0},{2,1},{3,2},{4,3},{5,4},{6,5},{7,6},{9,8},{10,9},{11,10},{12... | collective-permute-start | bytes 1413128 | tf_op jit(solution)/shard_map/ppermute | solution.py:257
  112.3 1.8 %copy-start.2 = (f32[896,8,128]{2,1,0:T(8,128)}, f32[896,8,128]{2,1,0:T(8,128)S(1)}, u32[]{:S(2)}) copy-start(f32[896,8,128]{2,1,0:T(8,128)S(1)} %all_to_all.5.arrived_ref) | copy-start | bytes 11010052

commit v2 on v1

v2 whole, which is shorter than its diff:
```python
import jax
import jax.numpy as jnp
from jax import lax
from jax.experimental import pallas as pl
from jax.experimental.pallas import tpu as pltpu
from jax.sharding import PartitionSpec as P

f32 = jnp.float32
N = 16
R = 4
E = N + 2 * R
W = 128
DEV = 128
CAP = 6
TILES = CAP + 1
SLOTS = 256
BIG = 1e30
MIB = 1024 * 1024

REACH = (4, 3, 3, 4, 3, 4, 3, 3, 3, 3, 2)
STARTS = tuple(sum(REACH[:field]) for field in range(10))
LIMIT_SLAB = sum(REACH[:10])
SLABS = LIMIT_SLAB + 1
SIDE = 4 * N
SIDE_ROWS = 11 * SIDE
CORNER = 4 * 6
CORNER_ROWS = 10 * CORNER + 8


def limit_row(flags_ref, stress_ref, row):
    along = jnp.where(
        flags_ref[row : row + 1] == 1, stress_ref[row : row + 1], BIG
    )
    square = jnp.broadcast_to(along, (N, N))
    diagonal = lax.broadcasted_iota(jnp.int32, (N, N), 0) == lax.broadcasted_iota(
        jnp.int32, (N, N), 1
    )
    column = jnp.sum(jnp.where(diagonal, square, 0.0), axis=1, keepdims=True)
    return jnp.broadcast_to(column, (N, W))


def scaled_inverse(density):
    return 0.075 / density


def pack_cut(
    flags_hbm, stress_hbm, state_ref, density_ref, low_ref, high_ref, flags_ref, stress_ref, edges, sems
):
    copies = [
        pltpu.make_async_copy(flags_hbm, flags_ref, sems.at[20]),
        pltpu.make_async_copy(stress_hbm, stress_ref, sems.at[21]),
    ]
    for field in range(9):
        source = state_ref.at[3 + field if field < 6 else field - 6]
        reach, start = REACH[field], STARTS[field]
        for side, target in enumerate((low_ref, high_ref)):
            copies.append(
                pltpu.make_async_copy(
                    source.at[pl.ds(side * (N - reach), reach)],
                    target.at[pl.ds(start, reach)],
                    sems.at[2 * field + side],
                )
            )
    for side in range(2):
        copies.append(
            pltpu.make_async_copy(
                density_ref.at[pl.ds(side * (N - 3), 3)], edges.at[side], sems.at[18 + side]
            )
        )
    for copy in copies:
        copy.start()
    copies[0].wait()
    copies[1].wait()
    half = lax.broadcasted_iota(jnp.int32, (N, W), 1) < W // 2
    for side, target in enumerate((low_ref, high_ref)):
        at = side * (N - 2)
        target[LIMIT_SLAB] = jnp.where(
            half,
            limit_row(flags_ref, stress_ref, at),
            limit_row(flags_ref, stress_ref, at + 1),
        )
    for copy in copies[2:]:
        copy.wait()
    for side, target in enumerate((low_ref, high_ref)):
        for row in range(3):
            target[STARTS[9] + row] = scaled_inverse(edges[side, row])


def pack_depth(flags_ref, stress_ref, state_ref, density_ref, low_ref, high_ref):
    for field in range(11):
        for row in range(N):
            if field < 6:
                own = state_ref[3 + field, row]
            elif field < 9:
                own = state_ref[field - 6, row]
            elif field == 9:
                own = scaled_inverse(density_ref[row])
            else:
                own = limit_row(flags_ref, stress_ref, row)
            at = field * SIDE + row * 4
            low_ref[at : at + 4] = own[:4]
            high_ref[at : at + 4] = own[N - 4 :]


def cut_row(field, r, from_low_ref, from_high_ref):
    source = from_low_ref if r < R else from_high_ref
    if field == 10:
        slab = source[LIMIT_SLAB]
        first = lax.broadcasted_iota(jnp.int32, (N, W), 1) < W // 2
        wanted = first if r in (R - 2, R + N) else ~first
        return jnp.where(wanted, slab, pltpu.roll(slab, W // 2, 1))
    return source[STARTS[field] + (r - (R - REACH[field]) if r < R else r - R - N)]


def corner_at(field, r):
    if field == 10:
        return 10 * CORNER + (0 if r < R else 4)
    return field * CORNER + 4 * (r - 1 if r < R else r - R - N + 3)


def corner_rows(field):
    return (3, 20) if field == 10 else (1, 2, 3, 20, 21, 22)


def pack_corners(from_low_ref, from_high_ref, low_ref, high_ref):
    for field in range(11):
        for r in corner_rows(field):
            row = cut_row(field, r, from_low_ref, from_high_ref)
            at = corner_at(field, r)
            low_ref[at : at + 4] = row[:4]
            high_ref[at : at + 4] = row[N - 4 :]


def steps_and_remap(
    place_ref,
    flags_ref,
    yield_ref,
    state_ref,
    density_ref,
    cut_low_ref,
    cut_high_ref,
    side_low_ref,
    side_high_ref,
    corner_low_ref,
    corner_high_ref,
    labels_ref,
    weights_ref,
    after_ref,
    outgoing_ref,
    tension,
    velocity,
    inverse,
    limits,
    rows,
    after,
    held,
    sems,
    after_sem,
):
    per = 2 * N

    def fetch(cx):
        return pltpu.make_async_copy(
            weights_ref.at[pl.ds(cx * per, per)], held.at[pl.ds(cx * per, per)], sems.at[cx]
        )

    for cx in range(N):
        fetch(cx).start()

    for field in range(11):
        reach = REACH[field]
        for r in range(R - reach, R + N + reach):
            if r < R or r >= R + N:
                own = cut_row(field, r, cut_low_ref, cut_high_ref)
            elif field < 6:
                own = state_ref[3 + field, r - R]
            elif field < 9:
                own = state_ref[field - 6, r - R]
            elif field == 9:
                own = scaled_inverse(density_ref[r - R])
            else:
                own = limit_row(flags_ref, yield_ref, r - R)
            if R <= r < R + N:
                at = field * SIDE + 4 * (r - R)
                beside = (side_high_ref[at : at + 4], side_low_ref[at : at + 4])
            elif r in corner_rows(field):
                at = corner_at(field, r)
                beside = (corner_high_ref[at : at + 4], corner_low_ref[at : at + 4])
            else:
                beside = (jnp.zeros((8, W), f32),)
            if field < 6:
                target = tension.at[field, r]
            elif field < 9:
                target = velocity.at[field - 6, r]
            else:
                target = (inverse if field == 9 else limits).at[r]
            target[:N] = own
            target[N:] = jnp.concatenate(beside, 0)

    def label(i, carry):
        for j in range(8):
            owner = i * 8 + j
            outgoing_ref[owner * TILES + CAP] = jnp.broadcast_to(labels_ref[owner], (8, W))
        return carry

    lax.fori_loop(0, DEV // 8, label, 0)

    lane = lax.broadcasted_iota(jnp.int32, (E, W), 1)
    first, last = lane == 0, lane == W - 1

    def along_depth(x):
        return pltpu.roll(x, E - 1, 0) - pltpu.roll(x, 1, 0)

    def along_width(x):
        up = jnp.where(last, 0.0, pltpu.roll(x, W - 1, 1))
        down = jnp.where(first, 0.0, pltpu.roll(x, 1, 1))
        return up - down

    def new_velocity(r):
        def along_cut(field):
            return tension[field, r + 1] - tension[field, r - 1]

        scale = inverse[r]
        xy, yz, xz = tension[3, r], tension[4, r], tension[5, r]
        return (
            velocity[0, r] + (along_cut(0) + along_depth(xy) + along_width(xz)) * scale,
            velocity[1, r] + (along_cut(3) + along_depth(tension[1, r]) + along_width(yz)) * scale,
            velocity[2, r] + (along_cut(5) + along_depth(yz) + along_width(tension[2, r])) * scale,
        )

    def new_stress(r):
        vx, vy, vz = velocity[0, r], velocity[1, r], velocity[2, r]
        limit = limits[r]

        def along_cut(field):
            return velocity[field, r + 1] - velocity[field, r - 1]

        xx, yy, zz = along_cut(0), along_depth(vy), along_width(vz)
        bulk = 0.075 * (xx + yy + zz)
        sxx = tension[0, r] + (0.09 * xx + bulk)
        syy = tension[1, r] + (0.09 * yy + bulk)
        szz = tension[2, r] + (0.09 * zz + bulk)
        sxy = tension[3, r] + 0.045 * (along_depth(vx) + along_cut(1))
        syz = tension[4, r] + 0.045 * (along_width(vy) + along_depth(vz))
        sxz = tension[5, r] + 0.045 * (along_width(vx) + along_cut(2))
        p = (sxx + syy + szz) * (1.0 / 3.0)
        dxx, dyy, dzz = sxx - p, syy - p, szz - p
        square = 1.5 * (
            dxx * dxx + dyy * dyy + dzz * dzz + 2.0 * (sxy * sxy + syz * syz + sxz * sxz)
        )
        factor = jnp.minimum(1.0, limit * lax.rsqrt(square))
        inside = limit > 0.0
        new = (
            p + factor * dxx,
            p + factor * dyy,
            p + factor * dzz,
            factor * sxy,
            factor * syz,
            factor * sxz,
        )
        return [jnp.where(inside, x, 0.0) for x in new]

    def sweep(start, stop, update, target):
        def body(i, carry):
            at = [start + GROUP * i + j for j in range(GROUP)]
            results = [update(r) for r in at]
            for r, result in zip(at, results):
                for field, x in enumerate(result):
                    target[field, r] = x
            return carry

        whole = (stop - start) // GROUP
        lax.fori_loop(0, whole, body, 0)
        rest = range(start + whole * GROUP, stop)
        for r, result in zip(rest, [update(r) for r in rest]):
            for field, x in enumerate(result):
                target[field, r] = x

    sweep(1, 23, new_velocity, velocity)
    sweep(2, 22, new_stress, tension)
    sweep(3, 21, new_velocity, velocity)

    def finish(i, carry):
        at = [GROUP * i + j for j in range(GROUP)]
        results = [new_stress(cx + R) for cx in at]
        for cx, result in zip(at, results):
            fields = [velocity[f, cx + R] for f in range(3)] + result
            for field, x in enumerate(fields):
                own = x[:N]
                after[field, cx] = own
                rows[cx, pl.ds(field, N, stride=16)] = own
        return carry

    lax.fori_loop(0, N // GROUP, finish, 0)
    keep = pltpu.make_async_copy(after, after_ref, after_sem)
    keep.start()

    def remap(cx, carry):
        fetch(cx).wait()
        for cy in range(0, N, 2):
            one = rows[cx, cy * 16 : (cy + 1) * 16].astype(jnp.bfloat16)
            two = rows[cx, (cy + 1) * 16 : (cy + 2) * 16].astype(jnp.bfloat16)
            none = jnp.zeros((16, W), jnp.bfloat16)
            blocks = jnp.concatenate(
                [jnp.concatenate([one, none], 1), jnp.concatenate([none, two], 1)], 0
            )
            pair = cx * per + 2 * cy
            spread = jnp.concatenate(
                [
                    jnp.concatenate([held[pair], held[pair + 1]], 1),
                    jnp.concatenate([held[pair + 2], held[pair + 3]], 1),
                ],
                0,
            )
            result = jnp.dot(blocks, spread, preferred_element_type=f32)
            for k in range(4):
                place = place_ref[pair + k]
                base = (place >> 3) * TILES
                rank = place & 7
                part = result[16 * (k // 2) : 16 * (k // 2) + 9, W * (k % 2) : W * (k % 2 + 1)]
                outgoing_ref[base + rank] = part[:8]
                outgoing_ref[base + CAP, pl.ds(rank, 1)] = part[8:9]
        return carry

    lax.fori_loop(0, N, remap, 0)
    keep.wait()


GROUP = 4
PARTS = 6
ROOM = SLOTS + 8


def gather(arrived, out_ref, turned, slots, sem, *sums):
    main, rest = sums[:PARTS], sums[PARTS:]
    named = arrived[:, CAP, CAP, :].T[:8].astype(jnp.int32)
    turned[...] = jnp.where(named == 0, SLOTS, named - 1)
    copy = pltpu.make_async_copy(turned, slots, sem)
    copy.start()
    for k in range(PARTS):
        main[k][...] = jnp.zeros((8 * ROOM, W), f32)
        rest[k][...] = jnp.zeros((ROOM, W), f32)
    copy.wait()

    def sources(i, carry):
        for j in range(UNROLL):
            source = i * UNROLL + j
            for k in range(CAP):
                slot = slots[k, source]
                tile = pl.ds(pl.multiple_of(slot * 8, 8), 8)
                main[k][tile] += arrived[source, k]
                rest[k][pl.ds(slot, 1)] += arrived[source, CAP, k : k + 1]
        return carry

    lax.fori_loop(0, DEV // UNROLL, sources, 0)

    def total(parts, spot):
        one, two, three = (parts[k][spot] + parts[k + 3][spot] for k in range(3))
        return one + two + three

    def fold(i, carry):
        spot = pl.ds(pl.multiple_of(i * W, W), W)
        main[0][spot] = total(main, spot)
        return carry

    lax.fori_loop(0, 8 * SLOTS // W, fold, 0)
    for field in range(8):
        out_ref[field] = main[0][pl.ds(field, SLOTS, stride=8)]
    out_ref[8] = total(rest, pl.ds(0, SLOTS))


UNROLL = 4


def exchange(low, high, axis):
    count = lax.axis_size(axis)
    up = [(i, i + 1) for i in range(count - 1)]
    down = [(target, source) for source, target in up]
    return lax.ppermute(high, axis, up), lax.ppermute(low, axis, down)


VM = pl.BlockSpec(memory_space=pltpu.VMEM)
SM = pl.BlockSpec(memory_space=pltpu.SMEM)
HB = pl.BlockSpec(memory_space=pltpu.HBM)
SMALL = pltpu.CompilerParams(vmem_limit_bytes=8 * MIB)


def stay(x):
    return pltpu.with_memory_space_constraint(x, pltpu.HBM)


def both(rows):
    return (jax.ShapeDtypeStruct(rows + (W,), f32),) * 2


def on_device(
    initial_state, density, yield_flags, yield_stress, crossing_weights, new_owner, new_slot
):
    low, high = pl.pallas_call(
        pack_cut,
        out_shape=both((SLABS, N)),
        in_specs=[HB] * 4,
        out_specs=(VM, VM),
        scratch_shapes=[
            pltpu.VMEM((N, N), jnp.int32),
            pltpu.VMEM((N, N), f32),
            pltpu.VMEM((2, 3, N, W), f32),
            pltpu.SemaphoreType.DMA((22,)),
        ],
        compiler_params=SMALL,
        name="pack_cut",
    )(*(stay(x) for x in (yield_flags, yield_stress, initial_state, density)))
    cut_low, cut_high = exchange(low, high, "cut")
    low, high = pl.pallas_call(
        pack_depth,
        out_shape=both((SIDE_ROWS,)),
        in_specs=[VM] * 4,
        out_specs=(VM, VM),
        compiler_params=SMALL,
        name="pack_depth",
    )(yield_flags, yield_stress, initial_state, density)
    side_low, side_high = exchange(low, high, "depth")
    low, high = pl.pallas_call(
        pack_corners,
        out_shape=both((CORNER_ROWS,)),
        in_specs=[VM] * 2,
        out_specs=(VM, VM),
        compiler_params=SMALL,
        name="pack_corners",
    )(cut_low, cut_high)
    corner_low, corner_high = exchange(low, high, "depth")

    owners = new_owner[:, 0]
    hits = (owners[:, None] == jnp.arange(DEV, dtype=jnp.int32)[None, :]).astype(jnp.int32)
    rank = jnp.sum((jnp.cumsum(hits, 0) - hits) * hits, 1)
    place = owners * 8 + rank
    by_rank = jnp.where(
        rank[:, None] == jnp.arange(W, dtype=jnp.int32)[None, :], new_slot[:, None] + 1, 0
    )
    labels = lax.dot_general(
        hits.astype(jnp.bfloat16),
        by_rank.astype(jnp.bfloat16),
        (((0,), (0,)), ((), ())),
        preferred_element_type=f32,
    )

    state_after, outgoing = pl.pallas_call(
        steps_and_remap,
        out_shape=(
            jax.ShapeDtypeStruct((9, N, N, W), f32),
            jax.ShapeDtypeStruct((DEV * TILES, 8, W), f32),
        ),
        in_specs=[SM] + [VM] * 11 + [HB],
        out_specs=(HB, VM),
        scratch_shapes=[
            pltpu.VMEM((6, E, E, W), f32),
            pltpu.VMEM((3, E, E, W), f32),
            pltpu.VMEM((E, E, W), f32),
            pltpu.VMEM((E, E, W), f32),
            pltpu.VMEM((N, N * 16, W), f32),
            pltpu.VMEM((9, N, N, W), f32),
            pltpu.VMEM((2 * N * N, W, W), jnp.bfloat16),
            pltpu.SemaphoreType.DMA((N,)),
            pltpu.SemaphoreType.DMA,
        ],
        compiler_params=pltpu.CompilerParams(vmem_limit_bytes=40 * MIB),
        name="steps_and_remap",
    )(
        place,
        yield_flags,
        yield_stress,
        initial_state,
        density,
        cut_low,
        cut_high,
        side_low,
        side_high,
        corner_low,
        corner_high,
        labels[:, None, :],
        stay(crossing_weights),
    )
    arrived = lax.all_to_all(outgoing, ("cut", "depth"), split_axis=0, concat_axis=0, tiled=True)
    new_integrals = pl.pallas_call(
        gather,
        out_shape=jax.ShapeDtypeStruct((9, SLOTS, W), f32),
        in_specs=[VM],
        out_specs=VM,
        scratch_shapes=[
            pltpu.VMEM((8, W), jnp.int32),
            pltpu.SMEM((8, W), jnp.int32),
            pltpu.SemaphoreType.DMA,
        ]
        + [pltpu.VMEM((8 * ROOM, W), f32)] * PARTS
        + [pltpu.VMEM((ROOM, W), f32)] * PARTS,
        compiler_params=pltpu.CompilerParams(vmem_limit_bytes=24 * MIB),
        name="gather",
    )(arrived.reshape(DEV, TILES, 8, W))
    return (state_after, new_integrals.transpose(1, 0, 2))


def solution(mesh):
    return jax.shard_map(
        on_device,
        mesh=mesh,
        in_specs=(
            P(None, "cut", "depth", None),
            P("cut", "depth", None),
            P("cut", "depth"),
            P("cut", "depth"),
            P(("cut", "depth"), None, None),
            P(("cut", "depth"), None),
            P(("cut", "depth")),
        ),
        out_specs=(P(None, "cut", "depth", None), P(("cut", "depth"), None, None)),
        check_vma=False,
    )
```

time: 121 us -> 104 us (0.86)
  Pallas kernels: 27.7 us -> 15.8 us
  waiting for transfers between devices: 14 us -> 4.28 us
  starting transfers between devices: 12.5 us -> 17.1 us
    pallas_call x1, Pallas kernels: 19 us -> 9.23 us  [on_device(): pl.pallas_call(steps_and_remap, out_shape=(jax.ShapeDtypeStruct((9, N, N,...]
    ppermute x4 -> x6, waiting for transfers between devices: 14 us -> 4.28 us  [exchange(): return (lax.ppermute(high, axis, up), lax.ppermute(low, axis, down))]
    ppermute x4 -> x6, starting transfers between devices: 12.5 us -> 17.1 us  [exchange(): return (lax.ppermute(high, axis, up), lax.ppermute(low, axis, down))]
    pallas_call x1, Pallas kernels: 5.91 us -> 4.21 us  [on_device(): pl.pallas_call(gather, out_shape=jax.ShapeDtypeStruct((9, SLOTS, W), f32)...]
    unnamed x9 -> x21, local copies, waits for them, and re-layouts: 3.55 us -> 4.3 us
    pallas_call x2 -> x3, Pallas kernels: 2.72 us -> 2.32 us  [the longest x1 2.09 us: on_device(): pl.pallas_call(pack_cut, out_shape=both((SLABS, N)), in_specs=[HB] * 4, o...]
  transfers between devices with their start and end apart: 4 -> 6, of which waited for: 4 -> 1; matrix products, arithmetic and copies ran while one was open for 2% -> 3% of each run, Pallas kernels for 0% -> 0%
where the time goes in v2:
time: 104 us; the launch traced here: 103 us
  blocking collectives  57.6 us (55%)
  starting transfers between devices  17.1 us (16%)
  Pallas kernels  15.8 us (15%)
  local copies, waits for them, and re-layouts  5.11 us (5%)
  waiting for transfers between devices  4.28 us (4%)
  other arithmetic  2.13 us (2%)
    all_to_all x1, blocking collectives, on_device(): lax.all_to_all(outgoing, ('cut', 'depth'), split_axis=0, concat_axis=0, t...  57.6 us
    ppermute x6, starting transfers between devices, exchange(): return (lax.ppermute(high, axis, up), lax.ppermute(low, axis, down))  17.1 us
    pallas_call x1, Pallas kernels, on_device(): pl.pallas_call(steps_and_remap, out_shape=(jax.ShapeDtypeStruct((9, N, N,...  9.23 us
    unnamed x21, local copies, waits for them, and re-layouts  4.3 us
    ppermute x6, waiting for transfers between devices, exchange(): return (lax.ppermute(high, axis, up), lax.ppermute(low, axis, down))  4.28 us
    pallas_call x1, Pallas kernels, on_device(): pl.pallas_call(gather, out_shape=jax.ShapeDtypeStruct((9, SLOTS, W), f32)...  4.21 us
    pallas_call x1, Pallas kernels, on_device(): pl.pallas_call(pack_cut, out_shape=both((SLABS, N)), in_specs=[HB] * 4, o...  2.09 us
  transfers between devices with their start and end apart: 6, of which 1 were waited for; matrix products, arithmetic and copies ran while one was open for 3% of the time, Pallas kernels for 0%

profile of v2, /device:TPU:1, one launch (start us, length us, event | category | flops | bytes accessed | tf_op | source)
XLA Modules:
  0.0 103.3 jit_solution(8673287213498903726)
XLA Ops:
  0.6 0.0 copy-start.7
  0.6 0.0 copy-start.5
  0.7 0.0 copy-start.3
  0.7 0.0 copy-start.1
  0.7 0.0 copy-start.9
  0.7 2.1 %pack_cut.1 = (f32[34,16,128]{2,1,0:T(8,128)}, f32[34,16,128]{2,1,0:T(8,128)}) custom-call(s32[16,16]{1,0:T(8,128)} %flags_ref.3, f32[16,16]{1,0:T(8,128)} %yield_ref.1, f32[9,16,16,128]{3,2,1,0:T(8,128)} %state_ref.5, f32[16,16,128]{2,1,0:T(8,128)} %density_ref.5), custom_call_target="tpu_custom_call" | custom-call | tf_op jit(solution)/shard_map/pack_cut/pallas_call | solution.py:399
  2.8 4.0 %collective-permute-start = (f32[34,16,128]{2,1,0:T(8,128)}, f32[34,16,128]{2,1,0:T(8,128)S(1)}, u32[]{:S(2)}, u32[]{:S(2)}) collective-permute-start(f32[34,16,128]{2,1,0:T(8,128)} %get-tuple-element.10), channel_id=1, source_target_pairs={{0,8},{8,16},{16,24},{24,32},{32,40},{40,48},{48,56},{56,64},{64,7... | collective-permute-start | bytes 835592 | tf_op jit(solution)/shard_map/ppermute | solution.py:379
  6.8 1.3 %collective-permute-start.1 = (f32[34,16,128]{2,1,0:T(8,128)}, f32[34,16,128]{2,1,0:T(8,128)S(1)}, u32[]{:S(2)}, u32[]{:S(2)}) collective-permute-start(f32[34,16,128]{2,1,0:T(8,128)} %get-tuple-element.11), channel_id=1, source_target_pairs={{8,0},{16,8},{24,16},{32,24},{40,32},{48,40},{56,48},{64,56},{72,6... | collective-permute-start | bytes 835592 | tf_op jit(solution)/shard_map/ppermute | solution.py:379
  8.1 0.0 copy-start
  8.1 1.3 %copy-done = f32[9,16,16,128]{3,2,1,0:T(8,128)S(1)} copy-done((f32[9,16,16,128]{3,2,1,0:T(8,128)S(1)}, f32[9,16,16,128]{3,2,1,0:T(8,128)}, u32[]{:S(2)}) %copy-start) | copy-done | bytes 1179672
  9.3 0.0 copy-start.2
  9.3 0.9 copy-done.2
  10.2 0.0 copy-start.4
  10.2 0.7 copy-done.4
  10.9 0.0 copy-start.6
  10.9 0.7 copy-done.6
  11.6 0.1 pack_depth.1
  11.8 4.4 %collective-permute-start.2 = (f32[704,128]{1,0:T(8,128)S(1)}, f32[704,128]{1,0:T(8,128)S(1)}, u32[]{:S(2)}, u32[]{:S(2)}) collective-permute-start(f32[704,128]{1,0:T(8,128)S(1)} %get-tuple-element.12), channel_id=1, source_target_pairs={{0,1},{1,2},{2,3},{3,4},{4,5},{5,6},{6,7},{8,9},{9,10},{10,11},{11... | collective-permute-start | bytes 1081352 | tf_op jit(solution)/shard_map/ppermute | solution.py:379
  16.2 1.9 %collective-permute-start.3 = (f32[704,128]{1,0:T(8,128)S(1)}, f32[704,128]{1,0:T(8,128)S(1)}, u32[]{:S(2)}, u32[]{:S(2)}) collective-permute-start(f32[704,128]{1,0:T(8,128)S(1)} %get-tuple-element.13), channel_id=1, source_target_pairs={{1,0},{2,1},{3,2},{4,3},{5,4},{6,5},{7,6},{9,8},{10,9},{11,10},{12... | collective-permute-start | bytes 1081352 | tf_op jit(solution)/shard_map/ppermute | solution.py:379
  18.1 0.7 broadcast_add_fusion.1
  18.8 0.8 copy.10
  19.6 0.2 fusion.2
  19.8 0.0 copy-start.8
  19.8 0.7 copy-done.8
  20.5 1.0 broadcast_add_fusion
  21.5 0.0 copy-done.9
  21.5 0.2 fusion.1
  21.8 0.4 fusion.4
  22.2 0.0 collective-permute-done.from_low_ref.cut_low_ref
  22.2 0.0 collective-permute-done.1.from_high_ref.cut_high_ref
  22.2 0.1 pack_corners.1
  22.3 3.6 %collective-permute-start.4 = (f32[248,128]{1,0:T(8,128)S(1)}, f32[248,128]{1,0:T(8,128)S(1)}, u32[]{:S(2)}, u32[]{:S(2)}) collective-permute-start(f32[248,128]{1,0:T(8,128)S(1)} %get-tuple-element.14), channel_id=1, source_target_pairs={{0,1},{1,2},{2,3},{3,4},{4,5},{5,6},{6,7},{8,9},{9,10},{10,11},{11... | collective-permute-start | bytes 380936 | tf_op jit(solution)/shard_map/ppermute | solution.py:379
  26.0 1.9 %collective-permute-start.5 = (f32[248,128]{1,0:T(8,128)S(1)}, f32[248,128]{1,0:T(8,128)S(1)}, u32[]{:S(2)}, u32[]{:S(2)}) collective-permute-start(f32[248,128]{1,0:T(8,128)S(1)} %get-tuple-element.15), channel_id=1, source_target_pairs={{1,0},{2,1},{3,2},{4,3},{5,4},{6,5},{7,6},{9,8},{10,9},{11,10},{12... | collective-permute-start | bytes 380936 | tf_op jit(solution)/shard_map/ppermute | solution.py:379
  27.9 0.0 collective-permute-done.2.side_low_ref
  27.9 0.0 collective-permute-done.3.side_high_ref
  27.9 0.0 collective-permute-done.4.corner_low_ref
  27.9 4.3 %collective-permute-done.5.corner_high_ref = f32[248,128]{1,0:T(8,128)S(1)} collective-permute-done((f32[248,128]{1,0:T(8,128)S(1)}, f32[248,128]{1,0:T(8,128)S(1)}, u32[]{:S(2)}, u32[]{:S(2)}) %collective-permute-start.5) | collective-permute-done | bytes 127008 | tf_op jit(solution)/shard_map/ppermute | solution.py:379
  32.2 0.0 copy-done.7
  32.2 0.0 copy-done.5
  32.2 0.0 copy-done.3
  32.2 0.0 copy-done.1
  32.2 9.2 %steps_and_remap.1 = (f32[9,16,16,128]{3,2,1,0:T(8,128)}, f32[896,8,128]{2,1,0:T(8,128)S(1)}) custom-call(s32[512]{0:T(512)S(1)} %multiply_add_fusion.place_ref, s32[16,16]{1,0:T(8,128)S(1)} %copy-done.5, f32[16,16]{1,0:T(8,128)S(1)} %copy-done.7, f32[9,16,16,128]{3,2,1,0:T(8,128)S(1)} %copy-done.1, f32[16,16,128]{2,1,0:T(8,128)S(1)} %copy-done.3, ...), custom_call_target="tpu_custom_call" | custom-call | tf_op jit(solution)/shard_map/steps_and_remap/pallas_call | solution.py:447
  41.5 57.6 %all_to_all.5 = f32[896,8,128]{2,1,0:T(8,128)S(1)} all-to-all(f32[896,8,128]{2,1,0:T(8,128)S(1)} %get-tuple-element.17), channel_id=1, replica_groups=mesh['cut'=16,'depth'=8] {'cut','depth'}, dimensions={0} | all-to-all | bytes 7340032 | tf_op jit(solution)/shard_map/all_to_all | solution.py:483
  99.1 4.2 %gather.1 = f32[9,256,128]{2,1,0:T(8,128)} custom-call(f32[128,7,8,128]{3,2,1,0:T(8,128)S(1)} %bitcast.14), custom_call_target="tpu_custom_call" | custom-call | tf_op jit(solution)/shard_map/gather/pallas_call | solution.py:484
  (6 shorter events, 0.1 us)
Async XLA Ops:
  0.6 31.6 %copy-start.7 = (f32[16,16]{1,0:T(8,128)S(1)}, f32[16,16]{1,0:T(8,128)}, u32[]{:S(2)}) copy-start(f32[16,16]{1,0:T(8,128)} %yield_ref.1) | copy-start | bytes 3076
  0.6 31.6 %copy-start.5 = (s32[16,16]{1,0:T(8,128)S(1)}, s32[16,16]{1,0:T(8,128)}, u32[]{:S(2)}) copy-start(s32[16,16]{1,0:T(8,128)} %flags_ref.3) | copy-start | bytes 3076
  0.7 31.6 %copy-start.3 = (f32[16,16,128]{2,1,0:T(8,128)S(1)}, f32[16,16,128]{2,1,0:T(8,128)}, u32[]{:S(2)}) copy-start(f32[16,16,128]{2,1,0:T(8,128)} %density_ref.5) | copy-start | bytes 393220
  0.7 31.6 %copy-start.1 = (f32[9,16,16,128]{3,2,1,0:T(8,128)S(1)}, f32[9,16,16,128]{3,2,1,0:T(8,128)}, u32[]{:S(2)}) copy-start(f32[9,16,16,128]{3,2,1,0:T(8,128)} %state_ref.5) | copy-start | bytes 3538948
  0.7 20.8 %copy-start.9 = (s32[512,1]{0,1:T(1,128)S(1)}, s32[512,1]{0,1:T(1,128)}, u32[]{:S(2)}) copy-start(s32[512,1]{0,1:T(1,128)} %param.12) | copy-start | bytes 6148
  2.8 19.4 %collective-permute-start = (f32[34,16,128]{2,1,0:T(8,128)}, f32[34,16,128]{2,1,0:T(8,128)S(1)}, u32[]{:S(2)}, u32[]{:S(2)}) collective-permute-start(f32[34,16,128]{2,1,0:T(8,128)} %get-tuple-element.10), channel_id=1, source_target_pairs={{0,8},{8,16},{16,24},{24,32},{32,40},{40,48},{48,56},{56,64},{64,7... | collective-permute-start | bytes 835592 | tf_op jit(solution)/shard_map/ppermute | solution.py:379
  6.8 15.5 %collective-permute-start.1 = (f32[34,16,128]{2,1,0:T(8,128)}, f32[34,16,128]{2,1,0:T(8,128)S(1)}, u32[]{:S(2)}, u32[]{:S(2)}) collective-permute-start(f32[34,16,128]{2,1,0:T(8,128)} %get-tuple-element.11), channel_id=1, source_target_pairs={{8,0},{16,8},{24,16},{32,24},{40,32},{48,40},{56,48},{64,56},{72,6... | collective-permute-start | bytes 835592 | tf_op jit(solution)/shard_map/ppermute | solution.py:379
  8.1 1.3 %copy-start = (f32[9,16,16,128]{3,2,1,0:T(8,128)S(1)}, f32[9,16,16,128]{3,2,1,0:T(8,128)}, u32[]{:S(2)}) copy-start(f32[9,16,16,128]{3,2,1,0:T(8,128)} %state_ref.5) | copy-start | bytes 3538948
  9.3 0.9 copy-start.2
  10.2 0.7 copy-start.4
  10.9 0.7 copy-start.6
  11.8 16.2 %collective-permute-start.2 = (f32[704,128]{1,0:T(8,128)S(1)}, f32[704,128]{1,0:T(8,128)S(1)}, u32[]{:S(2)}, u32[]{:S(2)}) collective-permute-start(f32[704,128]{1,0:T(8,128)S(1)} %get-tuple-element.12), channel_id=1, source_target_pairs={{0,1},{1,2},{2,3},{3,4},{4,5},{5,6},{6,7},{8,9},{9,10},{10,11},{11... | collective-permute-start | bytes 1081352 | tf_op jit(solution)/shard_map/ppermute | solution.py:379
  16.2 11.8 %collective-permute-start.3 = (f32[704,128]{1,0:T(8,128)S(1)}, f32[704,128]{1,0:T(8,128)S(1)}, u32[]{:S(2)}, u32[]{:S(2)}) collective-permute-start(f32[704,128]{1,0:T(8,128)S(1)} %get-tuple-element.13), channel_id=1, source_target_pairs={{1,0},{2,1},{3,2},{4,3},{5,4},{6,5},{7,6},{9,8},{10,9},{11,10},{12... | collective-permute-start | bytes 1081352 | tf_op jit(solution)/shard_map/ppermute | solution.py:379
  19.8 0.7 copy-start.8
  22.3 5.6 %collective-permute-start.4 = (f32[248,128]{1,0:T(8,128)S(1)}, f32[248,128]{1,0:T(8,128)S(1)}, u32[]{:S(2)}, u32[]{:S(2)}) collective-permute-start(f32[248,128]{1,0:T(8,128)S(1)} %get-tuple-element.14), channel_id=1, source_target_pairs={{0,1},{1,2},{2,3},{3,4},{4,5},{5,6},{6,7},{8,9},{9,10},{10,11},{11... | collective-permute-start | bytes 380936 | tf_op jit(solution)/shard_map/ppermute | solution.py:379
  26.0 6.2 %collective-permute-start.5 = (f32[248,128]{1,0:T(8,128)S(1)}, f32[248,128]{1,0:T(8,128)S(1)}, u32[]{:S(2)}, u32[]{:S(2)}) collective-permute-start(f32[248,128]{1,0:T(8,128)S(1)} %get-tuple-element.15), channel_id=1, source_target_pairs={{1,0},{2,1},{3,2},{4,3},{5,4},{6,5},{7,6},{9,8},{10,9},{11,10},{12... | collective-permute-start | bytes 380936 | tf_op jit(solution)/shard_map/ppermute | solution.py:379

commit v3 on v2

--- a/solution.py
+++ b/solution.py
@@ -21,10 +21,30 @@
 STARTS = tuple(sum(REACH[:field]) for field in range(10))
 LIMIT_SLAB = sum(REACH[:10])
 SLABS = LIMIT_SLAB + 1
-SIDE = 4 * N
-SIDE_ROWS = 11 * SIDE
-CORNER = 4 * 6
-CORNER_ROWS = 10 * CORNER + 8
+WIDTH = (3, 4, 3, 4, 4, 3, 3, 3, 3, 3, 2)
+RADIUS = (4,) * 6 + (3,) * 4 + (2,)
+
+
+def pieces(corners, at):
+    found = {}
+    for field in range(11):
+        for r in range(E):
+            beyond = max(R - r, r - (R + N - 1), 0)
+            width = WIDTH[field] if beyond == 0 else RADIUS[field] - beyond
+            if width > 0 and (beyond > 0) == corners:
+                found[field, r] = (width, at)
+                at += width
+    return found, at
+
+
+BESIDE, BESIDE_ROWS = pieces(False, 0)
+CORNERS, PIECE_ROWS = pieces(True, BESIDE_ROWS)
+PIECES = BESIDE | CORNERS
+SIDE_ROWS = -(-PIECE_ROWS // 8) * 8
+
+
+def is_odd(axis):
+    return lax.rem(lax.axis_index(axis), 2) == 1
 
 
 def limit_row(flags_ref, stress_ref, row):
@@ -44,8 +64,10 @@
 
 
 def pack_cut(
-    flags_hbm, stress_hbm, state_ref, density_ref, low_ref, high_ref, flags_ref, stress_ref, edges, sems
+    flags_hbm, stress_hbm, state_ref, density_ref, one_ref, two_ref, flags_ref, stress_ref, edges, sems
 ):
+    odd = lax.rem(lax.axis_index("cut"), 2)
+    tops = ((one_ref, odd), (two_ref, 1 - odd))
     copies = [
         pltpu.make_async_copy(flags_hbm, flags_ref, sems.at[20]),
         pltpu.make_async_copy(stress_hbm, stress_ref, sems.at[21]),
@@ -53,18 +75,18 @@
     for field in range(9):
         source = state_ref.at[3 + field if field < 6 else field - 6]
         reach, start = REACH[field], STARTS[field]
-        for side, target in enumerate((low_ref, high_ref)):
+        for side, (target, top) in enumerate(tops):
             copies.append(
                 pltpu.make_async_copy(
-                    source.at[pl.ds(side * (N - reach), reach)],
+                    source.at[pl.ds(top * (N - reach), reach)],
                     target.at[pl.ds(start, reach)],
                     sems.at[2 * field + side],
                 )
             )
-    for side in range(2):
+    for side, (target, top) in enumerate(tops):
         copies.append(
             pltpu.make_async_copy(
-                density_ref.at[pl.ds(side * (N - 3), 3)], edges.at[side], sems.at[18 + side]
+                density_ref.at[pl.ds(top * (N - 3), 3)], edges.at[side], sems.at[18 + side]
             )
         )
     for copy in copies:
@@ -72,63 +94,92 @@
     copies[0].wait()
     copies[1].wait()
     half = lax.broadcasted_iota(jnp.int32, (N, W), 1) < W // 2
-    for side, target in enumerate((low_ref, high_ref)):
-        at = side * (N - 2)
-        target[LIMIT_SLAB] = jnp.where(
+    slabs = [
+        jnp.where(
             half,
-            limit_row(flags_ref, stress_ref, at),
-            limit_row(flags_ref, stress_ref, at + 1),
+            limit_row(flags_ref, stress_ref, row),
+            limit_row(flags_ref, stress_ref, row + 1),
         )
+        for row in (0, N - 2)
+    ]
+    for target, top in tops:
+        target[LIMIT_SLAB] = jnp.where(top == 1, slabs[1], slabs[0])
     for copy in copies[2:]:
         copy.wait()
-    for side, target in enumerate((low_ref, high_ref)):
+    for side, (target, top) in enumerate(tops):
         for row in range(3):
             target[STARTS[9] + row] = scaled_inverse(edges[side, row])
 
 
-def pack_depth(flags_ref, stress_ref, state_ref, density_ref, low_ref, high_ref):
-    for field in range(11):
-        for row in range(N):
-            if field < 6:
-                own = state_ref[3 + field, row]
-            elif field < 9:
-                own = state_ref[field - 6, row]
-            elif field == 9:
-                own = scaled_inverse(density_ref[row])
-            else:
-                own = limit_row(flags_ref, stress_ref, row)
-            at = field * SIDE + row * 4
-            low_ref[at : at + 4] = own[:4]
-            high_ref[at : at + 4] = own[N - 4 :]
-
-
-def cut_row(field, r, from_low_ref, from_high_ref):
-    source = from_low_ref if r < R else from_high_ref
+def cut_row(field, r, odd, one_ref, two_ref):
+    def came(slab):
+        one, two = one_ref[slab], two_ref[slab]
+        return jnp.where(odd, two, one) if r < R else jnp.where(odd, one, two)
+
     if field == 10:
-        slab = source[LIMIT_SLAB]
+        slab = came(LIMIT_SLAB)
         first = lax.broadcasted_iota(jnp.int32, (N, W), 1) < W // 2
         wanted = first if r in (R - 2, R + N) else ~first
         return jnp.where(wanted, slab, pltpu.roll(slab, W // 2, 1))
-    return source[STARTS[field] + (r - (R - REACH[field]) if r < R else r - R - N)]
-
-
-def corner_at(field, r):
-    if field == 10:
-        return 10 * CORNER + (0 if r < R else 4)
-    return field * CORNER + 4 * (r - 1 if r < R else r - R - N + 3)
-
-
-def corner_rows(field):
-    return (3, 20) if field == 10 else (1, 2, 3, 20, 21, 22)
-
-
-def pack_corners(from_low_ref, from_high_ref, low_ref, high_ref):
-    for field in range(11):
-        for r in corner_rows(field):
-            row = cut_row(field, r, from_low_ref, from_high_ref)
-            at = corner_at(field, r)
-            low_ref[at : at + 4] = row[:4]
-            high_ref[at : at + 4] = row[N - 4 :]
+    return came(STARTS[field] + (r - (R - REACH[field]) if r < R else r - R - N))
+
+
+def own_row(field, row, flags_ref, yield_ref, state_ref, density_ref):
+    if field < 6:
+        return state_ref[3 + field, row]
+    if field < 9:
+        return state_ref[field - 6, row]
+    if field == 9:
+        return scaled_inverse(density_ref[row])
+    return limit_row(flags_ref, yield_ref, row)
+
+
+def put_piece(row, width, at, odd, one_ref, two_ref):
+    low, high = row[:width], row[N - width :]
+    one_ref[at : at + width] = jnp.where(odd, high, low)
+    two_ref[at : at + width] = jnp.where(odd, low, high)
+
+
+def pack_beside(
+    flags_hbm,
+    yield_hbm,
+    state_hbm,
+    density_hbm,
+    one_ref,
+    two_ref,
+    flags_ref,
+    yield_ref,
+    state_ref,
+    density_ref,
+    sems,
+):
+    pairs = (
+        (flags_hbm, flags_ref),
+        (yield_hbm, yield_ref),
+        (state_hbm, state_ref),
+        (density_hbm, density_ref),
+    )
+    copies = [
+        pltpu.make_async_copy(source, target, sems.at[k])
+        for k, (source, target) in enumerate(pairs)
+    ]
+    for copy in copies:
+        copy.start()
+    for copy in copies:
+        copy.wait()
+    odd = is_odd("depth")
+    for (field, r), (width, at) in BESIDE.items():
+        row = own_row(field, r - R, flags_ref, yield_ref, state_ref, density_ref)
+        put_piece(row, width, at, odd, one_ref, two_ref)
+
+
+def pack_corners(cut_one_ref, cut_two_ref, beside_one_ref, beside_two_ref, one_ref, two_ref):
+    one_ref[:BESIDE_ROWS] = beside_one_ref[...]
+    two_ref[:BESIDE_ROWS] = beside_two_ref[...]
+    odd_cut, odd = is_odd("cut"), is_odd("depth")
+    for (field, r), (width, at) in CORNERS.items():
+        row = cut_row(field, r, odd_cut, cut_one_ref, cut_two_ref)
+        put_piece(row, width, at, odd, one_ref, two_ref)
 
 
 def steps_and_remap(
@@ -137,12 +188,10 @@
     yield_ref,
     state_ref,
     density_ref,
-    cut_low_ref,
-    cut_high_ref,
-    side_low_ref,
-    side_high_ref,
-    corner_low_ref,
-    corner_high_ref,
+    cut_one_ref,
+    cut_two_ref,
+    side_one_ref,
+    side_two_ref,
     labels_ref,
     weights_ref,
     after_ref,
@@ -167,27 +216,22 @@
     for cx in range(N):
         fetch(cx).start()
 
+    odd_cut, odd_depth = is_odd("cut"), is_odd("depth")
     for field in range(11):
         reach = REACH[field]
         for r in range(R - reach, R + N + reach):
-            if r < R or r >= R + N:
-                own = cut_row(field, r, cut_low_ref, cut_high_ref)
-            elif field < 6:
-                own = state_ref[3 + field, r - R]
-            elif field < 9:
-                own = state_ref[field - 6, r - R]
-            elif field == 9:
-                own = scaled_inverse(density_ref[r - R])
+            if R <= r < R + N:
+                own = own_row(field, r - R, flags_ref, yield_ref, state_ref, density_ref)
             else:
-                own = limit_row(flags_ref, yield_ref, r - R)
-            if R <= r < R + N:
-                at = field * SIDE + 4 * (r - R)
-                beside = (side_high_ref[at : at + 4], side_low_ref[at : at + 4])
-            elif r in corner_rows(field):
-                at = corner_at(field, r)
-                beside = (corner_high_ref[at : at + 4], corner_low_ref[at : at + 4])
+                own = cut_row(field, r, odd_cut, cut_one_ref, cut_two_ref)
+            width, at = PIECES.get((field, r), (0, 0))
+            if width == 0:
+                beside = [jnp.zeros((8, W), f32)]
             else:
-                beside = (jnp.zeros((8, W), f32),)
+                one, two = side_one_ref[at : at + width], side_two_ref[at : at + width]
+                beside = [jnp.where(odd_depth, one, two), jnp.where(odd_depth, two, one)]
+                if width < 4:
+                    beside.insert(1, jnp.zeros((8 - 2 * width, W), f32))
             if field < 6:
                 target = tension.at[field, r]
             elif field < 9:
@@ -372,11 +416,14 @@
 UNROLL = 4
 
 
-def exchange(low, high, axis):
+def exchange(one, two, axis):
     count = lax.axis_size(axis)
-    up = [(i, i + 1) for i in range(count - 1)]
-    down = [(target, source) for source, target in up]
-    return lax.ppermute(high, axis, up), lax.ppermute(low, axis, down)
+
+    def swap(first):
+        pairs = [(i, i + 1) for i in range(first, count - 1, 2)]
+        return pairs + [(high, low) for low, high in pairs]
+
+    return lax.ppermute(one, axis, swap(1)), lax.ppermute(two, axis, swap(0))
 
 
 VM = pl.BlockSpec(memory_space=pltpu.VMEM)
@@ -396,7 +443,8 @@
 def on_device(
     initial_state, density, yield_flags, yield_stress, crossing_weights, new_owner, new_slot
 ):
-    low, high = pl.pallas_call(
+    given = [stay(x) for x in (yield_flags, yield_stress, initial_state, density)]
+    one, two = pl.pallas_call(
         pack_cut,
         out_shape=both((SLABS, N)),
         in_specs=[HB] * 4,
@@ -409,26 +457,32 @@
         ],
         compiler_params=SMALL,
         name="pack_cut",
-    )(*(stay(x) for x in (yield_flags, yield_stress, initial_state, density)))
-    cut_low, cut_high = exchange(low, high, "cut")
-    low, high = pl.pallas_call(
-        pack_depth,
+    )(*given)
+    cut_one, cut_two = exchange(one, two, "cut")
+    beside_one, beside_two = pl.pallas_call(
+        pack_beside,
+        out_shape=both((BESIDE_ROWS,)),
+        in_specs=[HB] * 4,
+        out_specs=(VM, VM),
+        scratch_shapes=[
+            pltpu.VMEM((N, N), jnp.int32),
+            pltpu.VMEM((N, N), f32),
+            pltpu.VMEM((9, N, N, W), f32),
+            pltpu.VMEM((N, N, W), f32),
+            pltpu.SemaphoreType.DMA((4,)),
+        ],
+        compiler_params=SMALL,
+        name="pack_beside",
+    )(*given)
+    one, two = pl.pallas_call(
+        pack_corners,
         out_shape=both((SIDE_ROWS,)),
         in_specs=[VM] * 4,
         out_specs=(VM, VM),
         compiler_params=SMALL,
-        name="pack_depth",
-    )(yield_flags, yield_stress, initial_state, density)
-    side_low, side_high = exchange(low, high, "depth")
-    low, high = pl.pallas_call(
-        pack_corners,
-        out_shape=both((CORNER_ROWS,)),
-        in_specs=[VM] * 2,
-        out_specs=(VM, VM),
-        compiler_params=SMALL,
         name="pack_corners",
-    )(cut_low, cut_high)
-    corner_low, corner_high = exchange(low, high, "depth")
+    )(cut_one, cut_two, beside_one, beside_two)
+    side_one, side_two = exchange(one, two, "depth")
 
     owners = new_owner[:, 0]
     hits = (owners[:, None] == jnp.arange(DEV, dtype=jnp.int32)[None, :]).astype(jnp.int32)
@@ -450,7 +504,7 @@
             jax.ShapeDtypeStruct((9, N, N, W), f32),
             jax.ShapeDtypeStruct((DEV * TILES, 8, W), f32),
         ),
-        in_specs=[SM] + [VM] * 11 + [HB],
+        in_specs=[SM] + [VM] * 9 + [HB],
         out_specs=(HB, VM),
         scratch_shapes=[
             pltpu.VMEM((6, E, E, W), f32),
@@ -471,12 +525,10 @@
         yield_stress,
         initial_state,
         density,
-        cut_low,
-        cut_high,
-        side_low,
-        side_high,
-        corner_low,
-        corner_high,
+        cut_one,
+        cut_two,
+        side_one,
+        side_two,
         labels[:, None, :],
         stay(crossing_weights),
     )

time: 104 us -> 94.9 us (0.913)
  starting transfers between devices: 17.1 us -> 10.3 us
  local copies, waits for them, and re-layouts: 5.11 us -> 0.85 us
  waiting for transfers between devices: 4.28 us -> 6.75 us
    ppermute x6 -> x4, starting transfers between devices: 17.1 us -> 10.3 us  [exchange(): return (lax.ppermute(one, axis, swap(1)), lax.ppermute(two, axis, swap(0)))]
    unnamed x21 -> x13, local copies, waits for them, and re-layouts: 4.3 us -> 0.04 us
    ppermute x6 -> x4, waiting for transfers between devices: 4.28 us -> 6.75 us  [exchange(): return (lax.ppermute(one, axis, swap(1)), lax.ppermute(two, axis, swap(0)))]
    pallas_call x2, Pallas kernels: 0.23 us -> 1.66 us  [the longest x1 1.57 us: on_device(): pl.pallas_call(pack_beside, out_shape=both((BESIDE_ROWS,)), in_specs=[HB]...]
  transfers between devices with their start and end apart: 6 -> 4, of which waited for: 1 -> 2; matrix products, arithmetic and copies ran while one was open for 3% -> 3% of each run, Pallas kernels for 0% -> 2%
where the time goes in v3:
time: 94.9 us; the launch traced here: 94.6 us
  blocking collectives  57.8 us (61%)
  Pallas kernels  16.4 us (17%)
  starting transfers between devices  10.3 us (11%)
  waiting for transfers between devices  6.75 us (7%)
  other arithmetic  1.18 us (1%)
    all_to_all x1, blocking collectives, on_device(): lax.all_to_all(outgoing, ('cut', 'depth'), split_axis=0, concat_axis=0, t...  57.8 us
    ppermute x4, starting transfers between devices, exchange(): return (lax.ppermute(one, axis, swap(1)), lax.ppermute(two, axis, swap(0)))  10.3 us
    pallas_call x1, Pallas kernels, on_device(): pl.pallas_call(steps_and_remap, out_shape=(jax.ShapeDtypeStruct((9, N, N,...  9.27 us
    ppermute x4, waiting for transfers between devices, exchange(): return (lax.ppermute(one, axis, swap(1)), lax.ppermute(two, axis, swap(0)))  6.75 us
    pallas_call x1, Pallas kernels, on_device(): pl.pallas_call(gather, out_shape=jax.ShapeDtypeStruct((9, SLOTS, W), f32)...  4.21 us
  transfers between devices with their start and end apart: 4, of which 2 were waited for; matrix products, arithmetic and copies ran while one was open for 3% of the time, Pallas kernels for 2%

profile of v3, /device:TPU:1, one launch (start us, length us, event | category | flops | bytes accessed | tf_op | source)
XLA Modules:
  0.0 94.6 jit_solution(3240026263823613373)
XLA Ops:
  0.6 0.0 copy-start.3
  0.6 0.0 copy-start.2
  0.7 0.0 copy-start.1
  0.7 0.0 copy-start
  0.7 0.0 copy-start.4
  0.7 0.0 copy-start.5
  0.7 1.3 %pack_cut.1 = (f32[34,16,128]{2,1,0:T(8,128)S(1)}, f32[34,16,128]{2,1,0:T(8,128)S(1)}) custom-call(s32[16,16]{1,0:T(8,128)} %flags_ref.1, f32[16,16]{1,0:T(8,128)} %yield_ref.1, f32[9,16,16,128]{3,2,1,0:T(8,128)} %state_ref.3, f32[16,16,128]{2,1,0:T(8,128)} %density_ref.3), custom_call_target="tpu_custom_call" | custom-call | tf_op jit(solution)/shard_map/pack_cut/pallas_call | solution.py:447
  2.0 0.7 collective-permute-start
  2.7 4.6 %collective-permute-start.1 = (f32[34,16,128]{2,1,0:T(8,128)S(1)}, f32[34,16,128]{2,1,0:T(8,128)S(1)}, u32[]{:S(2)}, u32[]{:S(2)}) collective-permute-start(f32[34,16,128]{2,1,0:T(8,128)S(1)} %get-tuple-element.11), channel_id=1, source_target_pairs={{0,8},{16,24},{32,40},{48,56},{64,72},{80,88},{96,104},{112,120},{... | collective-permute-start | bytes 835592 | tf_op jit(solution)/shard_map/ppermute | solution.py:426
  7.2 0.8 copy.10
  8.0 0.2 fusion.2
  8.3 0.9 fusion.1
  9.3 1.6 %pack_beside.1 = (f32[560,128]{1,0:T(8,128)S(1)}, f32[560,128]{1,0:T(8,128)S(1)}) custom-call(s32[16,16]{1,0:T(8,128)} %flags_ref.1, f32[16,16]{1,0:T(8,128)} %yield_ref.1, f32[9,16,16,128]{3,2,1,0:T(8,128)} %state_ref.3, f32[16,16,128]{2,1,0:T(8,128)} %density_ref.3), custom_call_target="tpu_custom_call" | custom-call | tf_op jit(solution)/shard_map/pack_beside/pallas_call | solution.py:462
  10.8 0.0 copy-done.4
  10.9 0.0 collective-permute-done.cut_one_ref
  10.9 2.4 %collective-permute-done.1.cut_two_ref = f32[34,16,128]{2,1,0:T(8,128)S(1)} collective-permute-done((f32[34,16,128]{2,1,0:T(8,128)S(1)}, f32[34,16,128]{2,1,0:T(8,128)S(1)}, u32[]{:S(2)}, u32[]{:S(2)}) %collective-permute-start.1) | collective-permute-done | bytes 278560 | tf_op jit(solution)/shard_map/ppermute | solution.py:426
  13.3 0.1 pack_corners.1
  13.4 5.0 %collective-permute-start.2 = (f32[664,128]{1,0:T(8,128)S(1)}, f32[664,128]{1,0:T(8,128)S(1)}, u32[]{:S(2)}, u32[]{:S(2)}) collective-permute-start(f32[664,128]{1,0:T(8,128)S(1)} %get-tuple-element.14), channel_id=1, source_target_pairs={{1,2},{3,4},{5,6},{2,1},{4,3},{6,5},{9,10},{11,12},{13,14},{10,9},... | collective-permute-start | bytes 1019912 | tf_op jit(solution)/shard_map/ppermute | solution.py:426
  18.4 0.1 collective-permute-start.3
  18.5 0.0 copy-done.5
  18.5 0.4 fusion.4
  18.9 4.3 %collective-permute-done.2.side_one_ref = f32[664,128]{1,0:T(8,128)S(1)} collective-permute-done((f32[664,128]{1,0:T(8,128)S(1)}, f32[664,128]{1,0:T(8,128)S(1)}, u32[]{:S(2)}, u32[]{:S(2)}) %collective-permute-start.2) | collective-permute-done | bytes 340000 | tf_op jit(solution)/shard_map/ppermute | solution.py:426
  23.3 0.0 collective-permute-done.3.side_two_ref
  23.3 0.0 copy-done.3
  23.3 0.0 copy-done.2
  23.3 0.0 copy-done.1
  23.3 0.0 copy-done
  23.3 9.3 %steps_and_remap.1 = (f32[9,16,16,128]{3,2,1,0:T(8,128)}, f32[896,8,128]{2,1,0:T(8,128)S(1)}) custom-call(s32[512]{0:T(512)S(1)} %multiply_add_fusion.place_ref, s32[16,16]{1,0:T(8,128)S(1)} %copy-done.2, f32[16,16]{1,0:T(8,128)S(1)} %copy-done.3, f32[9,16,16,128]{3,2,1,0:T(8,128)S(1)} %copy-done, f32[16,16,128]{2,1,0:T(8,128)S(1)} %copy-done.1, ...), custom_call_target="tpu_custom_call" | custom-call | tf_op jit(solution)/shard_map/steps_and_remap/pallas_call | solution.py:501
  32.6 57.8 %all_to_all.5 = f32[896,8,128]{2,1,0:T(8,128)S(1)} all-to-all(f32[896,8,128]{2,1,0:T(8,128)S(1)} %get-tuple-element.17), channel_id=1, replica_groups=mesh['cut'=16,'depth'=8] {'cut','depth'}, dimensions={0} | all-to-all | bytes 7340032 | tf_op jit(solution)/shard_map/all_to_all | solution.py:535
  90.4 4.2 %gather.1 = f32[9,256,128]{2,1,0:T(8,128)} custom-call(f32[128,7,8,128]{3,2,1,0:T(8,128)S(1)} %bitcast.14), custom_call_target="tpu_custom_call" | custom-call | tf_op jit(solution)/shard_map/gather/pallas_call | solution.py:536
  (8 shorter events, 0.1 us)
Async XLA Ops:
  0.6 22.6 %copy-start.3 = (f32[16,16]{1,0:T(8,128)S(1)}, f32[16,16]{1,0:T(8,128)}, u32[]{:S(2)}) copy-start(f32[16,16]{1,0:T(8,128)} %yield_ref.1) | copy-start | bytes 3076
  0.6 22.6 %copy-start.2 = (s32[16,16]{1,0:T(8,128)S(1)}, s32[16,16]{1,0:T(8,128)}, u32[]{:S(2)}) copy-start(s32[16,16]{1,0:T(8,128)} %flags_ref.1) | copy-start | bytes 3076
  0.7 22.6 %copy-start.1 = (f32[16,16,128]{2,1,0:T(8,128)S(1)}, f32[16,16,128]{2,1,0:T(8,128)}, u32[]{:S(2)}) copy-start(f32[16,16,128]{2,1,0:T(8,128)} %density_ref.3) | copy-start | bytes 393220
  0.7 22.6 %copy-start = (f32[9,16,16,128]{3,2,1,0:T(8,128)S(1)}, f32[9,16,16,128]{3,2,1,0:T(8,128)}, u32[]{:S(2)}) copy-start(f32[9,16,16,128]{3,2,1,0:T(8,128)} %state_ref.3) | copy-start | bytes 3538948
  0.7 10.2 %copy-start.4 = (s32[512,1]{0,1:T(1,128)S(1)}, s32[512,1]{0,1:T(1,128)}, u32[]{:S(2)}) copy-start(s32[512,1]{0,1:T(1,128)} %param.12) | copy-start | bytes 6148
  0.7 17.8 %copy-start.5 = (s32[512]{0:T(512)S(1)}, s32[512]{0:T(512)}, u32[]{:S(2)}) copy-start(s32[512]{0:T(512)} %param.13) | copy-start | bytes 6148
  2.0 8.9 %collective-permute-start = (f32[34,16,128]{2,1,0:T(8,128)S(1)}, f32[34,16,128]{2,1,0:T(8,128)S(1)}, u32[]{:S(2)}, u32[]{:S(2)}) collective-permute-start(f32[34,16,128]{2,1,0:T(8,128)S(1)} %get-tuple-element.10), channel_id=1, source_target_pairs={{8,16},{24,32},{40,48},{56,64},{72,80},{88,96},{104,112},{16,8},{3... | collective-permute-start | bytes 835592 | tf_op jit(solution)/shard_map/ppermute | solution.py:426
  2.7 10.6 %collective-permute-start.1 = (f32[34,16,128]{2,1,0:T(8,128)S(1)}, f32[34,16,128]{2,1,0:T(8,128)S(1)}, u32[]{:S(2)}, u32[]{:S(2)}) collective-permute-start(f32[34,16,128]{2,1,0:T(8,128)S(1)} %get-tuple-element.11), channel_id=1, source_target_pairs={{0,8},{16,24},{32,40},{48,56},{64,72},{80,88},{96,104},{112,120},{... | collective-permute-start | bytes 835592 | tf_op jit(solution)/shard_map/ppermute | solution.py:426
  13.4 9.9 %collective-permute-start.2 = (f32[664,128]{1,0:T(8,128)S(1)}, f32[664,128]{1,0:T(8,128)S(1)}, u32[]{:S(2)}, u32[]{:S(2)}) collective-permute-start(f32[664,128]{1,0:T(8,128)S(1)} %get-tuple-element.14), channel_id=1, source_target_pairs={{1,2},{3,4},{5,6},{2,1},{4,3},{6,5},{9,10},{11,12},{13,14},{10,9},... | collective-permute-start | bytes 1019912 | tf_op jit(solution)/shard_map/ppermute | solution.py:426
  18.4 4.9 %collective-permute-start.3 = (f32[664,128]{1,0:T(8,128)S(1)}, f32[664,128]{1,0:T(8,128)S(1)}, u32[]{:S(2)}, u32[]{:S(2)}) collective-permute-start(f32[664,128]{1,0:T(8,128)S(1)} %get-tuple-element.15), channel_id=1, source_target_pairs={{0,1},{2,3},{4,5},{6,7},{1,0},{3,2},{5,4},{7,6},{8,9},{10,11},{12,... | collective-permute-start | bytes 1019912 | tf_op jit(solution)/shard_map/ppermute | solution.py:426

commit v4 on v3

--- a/solution.py
+++ b/solution.py
@@ -193,6 +193,7 @@
     side_one_ref,
     side_two_ref,
     labels_ref,
+    ready_ref,
     weights_ref,
     after_ref,
     outgoing_ref,
@@ -200,7 +201,8 @@
     velocity,
     inverse,
     limits,
-    rows,
+    rows_even,
+    rows_odd,
     after,
     held,
     sems,
@@ -210,10 +212,12 @@
 
     def fetch(cx):
         return pltpu.make_async_copy(
-            weights_ref.at[pl.ds(cx * per, per)], held.at[pl.ds(cx * per, per)], sems.at[cx]
+            weights_ref.at[pl.ds(cx * per, per)],
+            held.at[pl.ds((cx - READY) * per, per)],
+            sems.at[cx - READY],
         )
 
-    for cx in range(N):
+    for cx in range(READY, N):
         fetch(cx).start()
 
     odd_cut, odd_depth = is_odd("cut"), is_odd("depth")
@@ -305,73 +309,72 @@
         return [jnp.where(inside, x, 0.0) for x in new]
 
     def sweep(start, stop, update, target):
-        def body(i, carry):
-            at = [start + GROUP * i + j for j in range(GROUP)]
-            results = [update(r) for r in at]
-            for r, result in zip(at, results):
+        for low in range(start, stop, GROUP):
+            at = range(low, min(low + GROUP, stop))
+            for r, result in zip(at, [update(r) for r in at]):
                 for field, x in enumerate(result):
                     target[field, r] = x
-            return carry
-
-        whole = (stop - start) // GROUP
-        lax.fori_loop(0, whole, body, 0)
-        rest = range(start + whole * GROUP, stop)
-        for r, result in zip(rest, [update(r) for r in rest]):
-            for field, x in enumerate(result):
-                target[field, r] = x
-
-    sweep(1, 23, new_velocity, velocity)
-    sweep(2, 22, new_stress, tension)
-    sweep(3, 21, new_velocity, velocity)
-
-    def finish(i, carry):
-        at = [GROUP * i + j for j in range(GROUP)]
+
+    def finish(i, target):
+        at = range(BATCH * i, BATCH * (i + 1))
         results = [new_stress(cx + R) for cx in at]
-        for cx, result in zip(at, results):
+        for j, (cx, result) in enumerate(zip(at, results)):
             fields = [velocity[f, cx + R] for f in range(3)] + result
             for field, x in enumerate(fields):
                 own = x[:N]
                 after[field, cx] = own
-                rows[cx, pl.ds(field, N, stride=16)] = own
-        return carry
-
-    lax.fori_loop(0, N // GROUP, finish, 0)
+                target[j, pl.ds(field, N, stride=16)] = own
+
+    def remap(i, source):
+        none = jnp.zeros((16, W), jnp.bfloat16)
+        for j in range(BATCH):
+            for cy in range(0, N, 2):
+                one = source[j, cy * 16 : (cy + 1) * 16].astype(jnp.bfloat16)
+                two = source[j, (cy + 1) * 16 : (cy + 2) * 16].astype(jnp.bfloat16)
+                blocks = jnp.concatenate(
+                    [jnp.concatenate([one, none], 1), jnp.concatenate([none, two], 1)], 0
+                )
+                pair = (BATCH * i + j) * per + 2 * cy
+                here, at = (ready_ref, pair) if BATCH * i < READY else (held, pair - READY * per)
+                spread = jnp.concatenate(
+                    [
+                        jnp.concatenate([here[at], here[at + 1]], 1),
+                        jnp.concatenate([here[at + 2], here[at + 3]], 1),
+                    ],
+                    0,
+                )
+                result = jnp.dot(blocks, spread, preferred_element_type=f32)
+                for k in range(4):
+                    place = place_ref[pair + k]
+                    base = (place >> 3) * TILES
+                    rank = place & 7
+                    row, column = 16 * (k // 2), W * (k % 2)
+                    part = result[row : row + 9, column : column + W]
+                    outgoing_ref[base + rank] = part[:8]
+                    outgoing_ref[base + CAP, pl.ds(rank, 1)] = part[8:9]
+
     keep = pltpu.make_async_copy(after, after_ref, after_sem)
-    keep.start()
-
-    def remap(cx, carry):
-        fetch(cx).wait()
-        for cy in range(0, N, 2):
-            one = rows[cx, cy * 16 : (cy + 1) * 16].astype(jnp.bfloat16)
-            two = rows[cx, (cy + 1) * 16 : (cy + 2) * 16].astype(jnp.bfloat16)
-            none = jnp.zeros((16, W), jnp.bfloat16)
-            blocks = jnp.concatenate(
-                [jnp.concatenate([one, none], 1), jnp.concatenate([none, two], 1)], 0
-            )
-            pair = cx * per + 2 * cy
-            spread = jnp.concatenate(
-                [
-                    jnp.concatenate([held[pair], held[pair + 1]], 1),
-                    jnp.concatenate([held[pair + 2], held[pair + 3]], 1),
-                ],
-                0,
-            )
-            result = jnp.dot(blocks, spread, preferred_element_type=f32)
-            for k in range(4):
-                place = place_ref[pair + k]
-                base = (place >> 3) * TILES
-                rank = place & 7
-                part = result[16 * (k // 2) : 16 * (k // 2) + 9, W * (k % 2) : W * (k % 2 + 1)]
-                outgoing_ref[base + rank] = part[:8]
-                outgoing_ref[base + CAP, pl.ds(rank, 1)] = part[8:9]
-        return carry
-
-    lax.fori_loop(0, N, remap, 0)
+    batches = N // BATCH
+    for i in range(batches + 1):
+        for cx in range(max(READY, BATCH * (i - 1)), BATCH * i):
+            fetch(cx).wait()
+        if i < batches:
+            end = R + BATCH * (i + 1)
+            sweep(end - BATCH + 3 if i else 1, end + 3, new_velocity, velocity)
+            sweep(end - BATCH + 2 if i else 2, end + 2, new_stress, tension)
+            sweep(end - BATCH + 1 if i else 3, end + 1, new_velocity, velocity)
+            finish(i, (rows_even, rows_odd)[i % 2])
+        if i == batches - 1:
+            keep.start()
+        if i > 0:
+            remap(i - 1, (rows_even, rows_odd)[(i - 1) % 2])
     keep.wait()
 
 
+BATCH = 4
+READY = 8
 GROUP = 4
-PARTS = 6
+PARTS = 3
 ROOM = SLOTS + 8
 
 
@@ -390,17 +393,17 @@
         for j in range(UNROLL):
             source = i * UNROLL + j
             for k in range(CAP):
+                part = k % PARTS
                 slot = slots[k, source]
                 tile = pl.ds(pl.multiple_of(slot * 8, 8), 8)
-                main[k][tile] += arrived[source, k]
-                rest[k][pl.ds(slot, 1)] += arrived[source, CAP, k : k + 1]
+                main[part][tile] += arrived[source, k]
+                rest[part][pl.ds(slot, 1)] += arrived[source, CAP, k : k + 1]
         return carry
 
     lax.fori_loop(0, DEV // UNROLL, sources, 0)
 
     def total(parts, spot):
-        one, two, three = (parts[k][spot] + parts[k + 3][spot] for k in range(3))
-        return one + two + three
+        return parts[0][spot] + parts[1][spot] + parts[2][spot]
 
     def fold(i, carry):
         spot = pl.ds(pl.multiple_of(i * W, W), W)
@@ -414,6 +417,20 @@
 
 
 UNROLL = 4
+
+
+def bring(weights_ref, ready_ref, sems):
+    part = READY * 2 * N // 8
+    copies = [
+        pltpu.make_async_copy(
+            weights_ref.at[pl.ds(k * part, part)], ready_ref.at[pl.ds(k * part, part)], sems.at[k]
+        )
+        for k in range(8)
+    ]
+    for copy in copies:
+        copy.start()
+    for copy in copies:
+        copy.wait()
 
 
 def exchange(one, two, axis):
@@ -482,7 +499,20 @@
         compiler_params=SMALL,
         name="pack_corners",
     )(cut_one, cut_two, beside_one, beside_two)
+    one, two, weights = lax.optimization_barrier((one, two, crossing_weights))
     side_one, side_two = exchange(one, two, "depth")
+    ready = pl.pallas_call(
+        bring,
+        out_shape=jax.ShapeDtypeStruct((READY * 2 * N, W, W), jnp.bfloat16),
+        in_specs=[HB],
+        out_specs=VM,
+        scratch_shapes=[pltpu.SemaphoreType.DMA((8,))],
+        compiler_params=pltpu.CompilerParams(vmem_limit_bytes=12 * MIB),
+        cost_estimate=pl.CostEstimate(
+            flops=0, bytes_accessed=READY * 2 * N * W * W * 2, transcendentals=0
+        ),
+        name="bring",
+    )(stay(weights))
 
     owners = new_owner[:, 0]
     hits = (owners[:, None] == jnp.arange(DEV, dtype=jnp.int32)[None, :]).astype(jnp.int32)
@@ -504,20 +534,21 @@
             jax.ShapeDtypeStruct((9, N, N, W), f32),
             jax.ShapeDtypeStruct((DEV * TILES, 8, W), f32),
         ),
-        in_specs=[SM] + [VM] * 9 + [HB],
+        in_specs=[SM] + [VM] * 10 + [HB],
         out_specs=(HB, VM),
         scratch_shapes=[
             pltpu.VMEM((6, E, E, W), f32),
             pltpu.VMEM((3, E, E, W), f32),
             pltpu.VMEM((E, E, W), f32),
             pltpu.VMEM((E, E, W), f32),
-            pltpu.VMEM((N, N * 16, W), f32),
+            pltpu.VMEM((BATCH, N * 16, W), f32),
+            pltpu.VMEM((BATCH, N * 16, W), f32),
             pltpu.VMEM((9, N, N, W), f32),
-            pltpu.VMEM((2 * N * N, W, W), jnp.bfloat16),
-            pltpu.SemaphoreType.DMA((N,)),
+            pltpu.VMEM(((N - READY) * 2 * N, W, W), jnp.bfloat16),
+            pltpu.SemaphoreType.DMA((N - READY,)),
             pltpu.SemaphoreType.DMA,
         ],
-        compiler_params=pltpu.CompilerParams(vmem_limit_bytes=40 * MIB),
+        compiler_params=pltpu.CompilerParams(vmem_limit_bytes=24 * MIB),
         name="steps_and_remap",
     )(
         place,
@@ -530,6 +561,7 @@
         side_one,
         side_two,
         labels[:, None, :],
+        ready,
         stay(crossing_weights),
     )
     arrived = lax.all_to_all(outgoing, ("cut", "depth"), split_axis=0, concat_axis=0, tiled=True)

time: 94.9 us -> 90.7 us (0.956)
  waiting for transfers between devices: 6.75 us -> 3.13 us
    pallas_call x1, Pallas kernels: 9.27 us -> 5.41 us  [on_device(): pl.pallas_call(steps_and_remap, out_shape=(jax.ShapeDtypeStruct((9, N, N,...]
    ppermute x4, waiting for transfers between devices: 6.75 us -> 3.13 us  [exchange(): return (lax.ppermute(one, axis, swap(1)), lax.ppermute(two, axis, swap(0)))]
    pallas_call x0 -> x1, Pallas kernels: none -> 3.57 us  [on_device(): pl.pallas_call(bring, out_shape=jax.ShapeDtypeStruct((READY * 2 * N, W, W...]
  transfers between devices with their start and end apart: 4 -> 4, of which waited for: 2 -> 2; matrix products, arithmetic and copies ran while one was open for 3% -> 3% of each run, Pallas kernels for 2% -> 6%
where the time goes in v4:
time: 90.7 us; the launch traced here: 90.4 us
  blocking collectives  57.9 us (64%)
  Pallas kernels  15.8 us (17%)
  starting transfers between devices  10.3 us (11%)
  waiting for transfers between devices  3.13 us (3%)
  other arithmetic  1.18 us (1%)
    all_to_all x1, blocking collectives, on_device(): lax.all_to_all(outgoing, ('cut', 'depth'), split_axis=0, concat_axis=0, t...  57.9 us
    ppermute x4, starting transfers between devices, exchange(): return (lax.ppermute(one, axis, swap(1)), lax.ppermute(two, axis, swap(0)))  10.3 us
    pallas_call x1, Pallas kernels, on_device(): pl.pallas_call(steps_and_remap, out_shape=(jax.ShapeDtypeStruct((9, N, N,...  5.41 us
    pallas_call x1, Pallas kernels, on_device(): pl.pallas_call(gather, out_shape=jax.ShapeDtypeStruct((9, SLOTS, W), f32)...  3.9 us
    pallas_call x1, Pallas kernels, on_device(): pl.pallas_call(bring, out_shape=jax.ShapeDtypeStruct((READY * 2 * N, W, W...  3.57 us
    ppermute x4, waiting for transfers between devices, exchange(): return (lax.ppermute(one, axis, swap(1)), lax.ppermute(two, axis, swap(0)))  3.13 us
  transfers between devices with their start and end apart: 4, of which 2 were waited for; matrix products, arithmetic and copies ran while one was open for 3% of the time, Pallas kernels for 6%

profile of v4, /device:TPU:1, one launch (start us, length us, event | category | flops | bytes accessed | tf_op | source)
XLA Modules:
  0.0 90.4 jit_solution(11180101760827187416)
XLA Ops:
  0.6 0.0 copy-start.4
  0.6 0.0 copy-start.5
  0.7 1.2 %pack_cut.1 = (f32[34,16,128]{2,1,0:T(8,128)S(1)}, f32[34,16,128]{2,1,0:T(8,128)S(1)}) custom-call(s32[16,16]{1,0:T(8,128)} %flags_ref.1, f32[16,16]{1,0:T(8,128)} %yield_ref.1, f32[9,16,16,128]{3,2,1,0:T(8,128)} %state_ref.3, f32[16,16,128]{2,1,0:T(8,128)} %density_ref.3), custom_call_target="tpu_custom_call" | custom-call | tf_op jit(solution)/shard_map/pack_cut/pallas_call | solution.py:464
  1.9 0.7 collective-permute-start
  2.6 4.6 %collective-permute-start.1 = (f32[34,16,128]{2,1,0:T(8,128)S(1)}, f32[34,16,128]{2,1,0:T(8,128)S(1)}, u32[]{:S(2)}, u32[]{:S(2)}) collective-permute-start(f32[34,16,128]{2,1,0:T(8,128)S(1)} %get-tuple-element.14), channel_id=1, source_target_pairs={{0,8},{16,24},{32,40},{48,56},{64,72},{80,88},{96,104},{112,120},{... | collective-permute-start | bytes 835592 | tf_op jit(solution)/shard_map/ppermute | solution.py:443
  7.1 0.8 copy.10
  7.9 0.2 fusion.2
  8.2 0.9 %fusion.1 = s32[512]{0:T(512)S(1)} fusion(s32[128,4,128]{0,2,1:T(8,128)S(1)} %copy.11, s32[512]{0:T(512)} %bitcast.20), kind=kLoop, calls=%fused_computation.3 | loop fusion | flops 327168 | bytes 266240 | tf_op jit(solution)/shard_map/reduce_sum | solution.py:519
  9.2 1.6 %pack_beside.1 = (f32[560,128]{1,0:T(8,128)S(1)}, f32[560,128]{1,0:T(8,128)S(1)}) custom-call(s32[16,16]{1,0:T(8,128)} %flags_ref.1, f32[16,16]{1,0:T(8,128)} %yield_ref.1, f32[9,16,16,128]{3,2,1,0:T(8,128)} %state_ref.3, f32[16,16,128]{2,1,0:T(8,128)} %density_ref.3), custom_call_target="tpu_custom_call" | custom-call | tf_op jit(solution)/shard_map/pack_beside/pallas_call | solution.py:479
  10.7 0.0 copy-done.4
  10.8 0.0 collective-permute-done.cut_one_ref
  10.8 2.4 %collective-permute-done.1.cut_two_ref = f32[34,16,128]{2,1,0:T(8,128)S(1)} collective-permute-done((f32[34,16,128]{2,1,0:T(8,128)S(1)}, f32[34,16,128]{2,1,0:T(8,128)S(1)}, u32[]{:S(2)}, u32[]{:S(2)}) %collective-permute-start.1) | collective-permute-done | bytes 278560 | tf_op jit(solution)/shard_map/ppermute | solution.py:443
  13.2 0.1 pack_corners.1
  13.3 5.0 %collective-permute-start.2 = (f32[664,128]{1,0:T(8,128)S(1)}, f32[664,128]{1,0:T(8,128)S(1)}, u32[]{:S(2)}, u32[]{:S(2)}) collective-permute-start(f32[664,128]{1,0:T(8,128)S(1)} %get-tuple-element.19), channel_id=1, source_target_pairs={{1,2},{3,4},{5,6},{2,1},{4,3},{6,5},{9,10},{11,12},{13,14},{10,9},... | collective-permute-start | bytes 1019912 | tf_op jit(solution)/shard_map/ppermute | solution.py:443
  18.3 0.1 collective-permute-start.3
  18.4 0.0 copy-done.5
  18.4 0.4 fusion.4
  18.8 0.0 copy-start
  18.9 0.0 copy-start.1
  18.9 0.0 copy-start.2
  18.9 0.0 copy-start.3
  18.9 3.6 %bring.1.ready_ref = bf16[256,128,128]{2,1,0:T(8,128)(2,1)S(1)} custom-call(bf16[512,128,128]{2,1,0:T(8,128)(2,1)} %weights_ref.2), custom_call_target="tpu_custom_call" | custom-call | bytes 8388608 | tf_op jit(solution)/shard_map/bring/pallas_call | solution.py:504
  22.5 0.7 collective-permute-done.2.side_one_ref
  23.2 0.0 collective-permute-done.3.side_two_ref
  23.2 0.0 copy-done
  23.2 0.0 copy-done.1
  23.2 0.0 copy-done.2
  23.2 0.0 copy-done.3
  23.2 5.4 %steps_and_remap.1 = (f32[9,16,16,128]{3,2,1,0:T(8,128)}, f32[896,8,128]{2,1,0:T(8,128)S(1)}) custom-call(s32[512]{0:T(512)S(1)} %multiply_add_fusion.place_ref, s32[16,16]{1,0:T(8,128)S(1)} %copy-done.2, f32[16,16]{1,0:T(8,128)S(1)} %copy-done.3, f32[9,16,16,128]{3,2,1,0:T(8,128)S(1)} %copy-done, f32[16,16,128]{2,1,0:T(8,128)S(1)} %copy-done.1, ...), custom_call_target="tpu_custom_call" | custom-call | tf_op jit(solution)/shard_map/steps_and_remap/pallas_call | solution.py:531
  28.6 57.9 %all_to_all.5 = f32[896,8,128]{2,1,0:T(8,128)S(1)} all-to-all(f32[896,8,128]{2,1,0:T(8,128)S(1)} %get-tuple-element.23), channel_id=1, replica_groups=mesh['cut'=16,'depth'=8] {'cut','depth'}, dimensions={0} | all-to-all | bytes 7340032 | tf_op jit(solution)/shard_map/all_to_all | solution.py:567
  86.5 3.9 %gather.1 = f32[9,256,128]{2,1,0:T(8,128)} custom-call(f32[128,7,8,128]{3,2,1,0:T(8,128)S(1)} %bitcast.14), custom_call_target="tpu_custom_call" | custom-call | tf_op jit(solution)/shard_map/gather/pallas_call | solution.py:568
  (8 shorter events, 0.1 us)
Async XLA Ops:
  0.6 10.1 %copy-start.4 = (s32[512,1]{0,1:T(1,128)S(1)}, s32[512,1]{0,1:T(1,128)}, u32[]{:S(2)}) copy-start(s32[512,1]{0,1:T(1,128)} %param.12) | copy-start | bytes 6148
  0.6 17.7 %copy-start.5 = (s32[512]{0:T(512)S(1)}, s32[512]{0:T(512)}, u32[]{:S(2)}) copy-start(s32[512]{0:T(512)} %param.13) | copy-start | bytes 6148
  1.9 8.9 %collective-permute-start = (f32[34,16,128]{2,1,0:T(8,128)S(1)}, f32[34,16,128]{2,1,0:T(8,128)S(1)}, u32[]{:S(2)}, u32[]{:S(2)}) collective-permute-start(f32[34,16,128]{2,1,0:T(8,128)S(1)} %get-tuple-element.13), channel_id=1, source_target_pairs={{8,16},{24,32},{40,48},{56,64},{72,80},{88,96},{104,112},{16,8},{3... | collective-permute-start | bytes 835592 | tf_op jit(solution)/shard_map/ppermute | solution.py:443
  2.6 10.6 %collective-permute-start.1 = (f32[34,16,128]{2,1,0:T(8,128)S(1)}, f32[34,16,128]{2,1,0:T(8,128)S(1)}, u32[]{:S(2)}, u32[]{:S(2)}) collective-permute-start(f32[34,16,128]{2,1,0:T(8,128)S(1)} %get-tuple-element.14), channel_id=1, source_target_pairs={{0,8},{16,24},{32,40},{48,56},{64,72},{80,88},{96,104},{112,120},{... | collective-permute-start | bytes 835592 | tf_op jit(solution)/shard_map/ppermute | solution.py:443
  13.3 9.9 %collective-permute-start.2 = (f32[664,128]{1,0:T(8,128)S(1)}, f32[664,128]{1,0:T(8,128)S(1)}, u32[]{:S(2)}, u32[]{:S(2)}) collective-permute-start(f32[664,128]{1,0:T(8,128)S(1)} %get-tuple-element.19), channel_id=1, source_target_pairs={{1,2},{3,4},{5,6},{2,1},{4,3},{6,5},{9,10},{11,12},{13,14},{10,9},... | collective-permute-start | bytes 1019912 | tf_op jit(solution)/shard_map/ppermute | solution.py:443
  18.3 4.9 %collective-permute-start.3 = (f32[664,128]{1,0:T(8,128)S(1)}, f32[664,128]{1,0:T(8,128)S(1)}, u32[]{:S(2)}, u32[]{:S(2)}) collective-permute-start(f32[664,128]{1,0:T(8,128)S(1)} %get-tuple-element.20), channel_id=1, source_target_pairs={{0,1},{2,3},{4,5},{6,7},{1,0},{3,2},{5,4},{7,6},{8,9},{10,11},{12,... | collective-permute-start | bytes 1019912 | tf_op jit(solution)/shard_map/ppermute | solution.py:443
  18.8 4.3 %copy-start = (f32[9,16,16,128]{3,2,1,0:T(8,128)S(1)}, f32[9,16,16,128]{3,2,1,0:T(8,128)}, u32[]{:S(2)}) copy-start(f32[9,16,16,128]{3,2,1,0:T(8,128)} %state_ref.3) | copy-start | bytes 3538948
  18.9 4.3 %copy-start.1 = (f32[16,16,128]{2,1,0:T(8,128)S(1)}, f32[16,16,128]{2,1,0:T(8,128)}, u32[]{:S(2)}) copy-start(f32[16,16,128]{2,1,0:T(8,128)} %density_ref.3) | copy-start | bytes 393220
  18.9 4.3 %copy-start.2 = (s32[16,16]{1,0:T(8,128)S(1)}, s32[16,16]{1,0:T(8,128)}, u32[]{:S(2)}) copy-start(s32[16,16]{1,0:T(8,128)} %flags_ref.1) | copy-start | bytes 3076
  18.9 4.3 %copy-start.3 = (f32[16,16]{1,0:T(8,128)S(1)}, f32[16,16]{1,0:T(8,128)}, u32[]{:S(2)}) copy-start(f32[16,16]{1,0:T(8,128)} %yield_ref.1) | copy-start | bytes 3076

commit v5 on v4

--- a/solution.py
+++ b/solution.py
@@ -41,6 +41,7 @@
 CORNERS, PIECE_ROWS = pieces(True, BESIDE_ROWS)
 PIECES = BESIDE | CORNERS
 SIDE_ROWS = -(-PIECE_ROWS // 8) * 8
+CORNER_ROWS = SIDE_ROWS - BESIDE_ROWS
 
 
 def is_odd(axis):
@@ -134,10 +135,10 @@
     return limit_row(flags_ref, yield_ref, row)
 
 
-def put_piece(row, width, at, odd, one_ref, two_ref):
+def put_piece(row, width, odd, one_ref, one_at, two_ref, two_at):
     low, high = row[:width], row[N - width :]
-    one_ref[at : at + width] = jnp.where(odd, high, low)
-    two_ref[at : at + width] = jnp.where(odd, low, high)
+    one_ref[one_at : one_at + width] = jnp.where(odd, high, low)
+    two_ref[two_at : two_at + width] = jnp.where(odd, low, high)
 
 
 def pack_beside(
@@ -170,16 +171,15 @@
     odd = is_odd("depth")
     for (field, r), (width, at) in BESIDE.items():
         row = own_row(field, r - R, flags_ref, yield_ref, state_ref, density_ref)
-        put_piece(row, width, at, odd, one_ref, two_ref)
-
-
-def pack_corners(cut_one_ref, cut_two_ref, beside_one_ref, beside_two_ref, one_ref, two_ref):
-    one_ref[:BESIDE_ROWS] = beside_one_ref[...]
+        put_piece(row, width, odd, one_ref, at, two_ref, at)
+
+
+def pack_corners(cut_one_ref, cut_two_ref, beside_two_ref, one_ref, two_ref):
     two_ref[:BESIDE_ROWS] = beside_two_ref[...]
     odd_cut, odd = is_odd("cut"), is_odd("depth")
     for (field, r), (width, at) in CORNERS.items():
         row = cut_row(field, r, odd_cut, cut_one_ref, cut_two_ref)
-        put_piece(row, width, at, odd, one_ref, two_ref)
+        put_piece(row, width, odd, one_ref, at - BESIDE_ROWS, two_ref, at)
 
 
 def steps_and_remap(
@@ -190,7 +190,8 @@
     density_ref,
     cut_one_ref,
     cut_two_ref,
-    side_one_ref,
+    beside_one_ref,
+    corner_one_ref,
     side_two_ref,
     labels_ref,
     ready_ref,
@@ -232,7 +233,11 @@
             if width == 0:
                 beside = [jnp.zeros((8, W), f32)]
             else:
-                one, two = side_one_ref[at : at + width], side_two_ref[at : at + width]
+                two = side_two_ref[at : at + width]
+                if at < BESIDE_ROWS:
+                    one = beside_one_ref[at : at + width]
+                else:
+                    one = corner_one_ref[at - BESIDE_ROWS : at - BESIDE_ROWS + width]
                 beside = [jnp.where(odd_depth, one, two), jnp.where(odd_depth, two, one)]
                 if width < 4:
                     beside.insert(1, jnp.zeros((8 - 2 * width, W), f32))
@@ -372,7 +377,7 @@
 
 
 BATCH = 4
-READY = 8
+READY = 4
 GROUP = 4
 PARTS = 3
 ROOM = SLOTS + 8
@@ -433,14 +438,9 @@
         copy.wait()
 
 
-def exchange(one, two, axis):
-    count = lax.axis_size(axis)
-
-    def swap(first):
-        pairs = [(i, i + 1) for i in range(first, count - 1, 2)]
-        return pairs + [(high, low) for low, high in pairs]
-
-    return lax.ppermute(one, axis, swap(1)), lax.ppermute(two, axis, swap(0))
+def exchange(x, axis, first):
+    pairs = [(i, i + 1) for i in range(first, lax.axis_size(axis) - 1, 2)]
+    return lax.ppermute(x, axis, pairs + [(high, low) for low, high in pairs])
 
 
 VM = pl.BlockSpec(memory_space=pltpu.VMEM)
@@ -475,7 +475,7 @@
         compiler_params=SMALL,
         name="pack_cut",
     )(*given)
-    cut_one, cut_two = exchange(one, two, "cut")
+    cut_one, cut_two = exchange(one, "cut", 1), exchange(two, "cut", 0)
     beside_one, beside_two = pl.pallas_call(
         pack_beside,
         out_shape=both((BESIDE_ROWS,)),
@@ -491,16 +491,19 @@
         compiler_params=SMALL,
         name="pack_beside",
     )(*given)
+    beside_one, beside_two, weights = lax.optimization_barrier(
+        (beside_one, beside_two, crossing_weights)
+    )
+    beside_one = exchange(beside_one, "depth", 1)
     one, two = pl.pallas_call(
         pack_corners,
-        out_shape=both((SIDE_ROWS,)),
-        in_specs=[VM] * 4,
+        out_shape=both((CORNER_ROWS,))[:1] + both((SIDE_ROWS,))[:1],
+        in_specs=[VM] * 3,
         out_specs=(VM, VM),
         compiler_params=SMALL,
         name="pack_corners",
-    )(cut_one, cut_two, beside_one, beside_two)
-    one, two, weights = lax.optimization_barrier((one, two, crossing_weights))
-    side_one, side_two = exchange(one, two, "depth")
+    )(cut_one, cut_two, beside_two)
+    corner_one, side_two = exchange(one, "depth", 1), exchange(two, "depth", 0)
     ready = pl.pallas_call(
         bring,
         out_shape=jax.ShapeDtypeStruct((READY * 2 * N, W, W), jnp.bfloat16),
@@ -534,7 +537,7 @@
             jax.ShapeDtypeStruct((9, N, N, W), f32),
             jax.ShapeDtypeStruct((DEV * TILES, 8, W), f32),
         ),
-        in_specs=[SM] + [VM] * 10 + [HB],
+        in_specs=[SM] + [VM] * 11 + [HB],
         out_specs=(HB, VM),
         scratch_shapes=[
             pltpu.VMEM((6, E, E, W), f32),
@@ -558,7 +561,8 @@
         density,
         cut_one,
         cut_two,
-        side_one,
+        beside_one,
+        corner_one,
         side_two,
         labels[:, None, :],
         ready,

time: 90.7 us -> 89.2 us (0.983)
  starting transfers between devices: 10.3 us -> 13.9 us
  waiting for transfers between devices: 3.13 us -> 0.01 us
  blocking collectives: 57.9 us -> 56.8 us
    ppermute x4 -> x5, starting transfers between devices: 10.3 us -> 13.9 us  [exchange(): return lax.ppermute(x, axis, pairs + [(high, low) for low, high in pairs])]
    ppermute x4 -> x5, waiting for transfers between devices: 3.13 us -> 0.01 us  [exchange(): return lax.ppermute(x, axis, pairs + [(high, low) for low, high in pairs])]
    pallas_call x1, Pallas kernels: 3.57 us -> 2.31 us  [on_device(): pl.pallas_call(bring, out_shape=jax.ShapeDtypeStruct((READY * 2 * N, W, W...]
    all_to_all x1, blocking collectives: 57.9 us -> 56.8 us  [on_device(): lax.all_to_all(outgoing, ('cut', 'depth'), split_axis=0, concat_axis=0, t...]
  transfers between devices with their start and end apart: 4 -> 5, of which waited for: 2 -> 0; matrix products, arithmetic and copies ran while one was open for 3% -> 2% of each run, Pallas kernels for 6% -> 4%
where the time goes in v5:
time: 89.2 us; the launch traced here: 88.8 us
  blocking collectives  56.8 us (64%)
  Pallas kernels  15.4 us (17%)
  starting transfers between devices  13.9 us (16%)
  local copies, waits for them, and re-layouts  0.99 us (1%)
    all_to_all x1, blocking collectives, on_device(): lax.all_to_all(outgoing, ('cut', 'depth'), split_axis=0, concat_axis=0, t...  56.8 us
    ppermute x5, starting transfers between devices, exchange(): return lax.ppermute(x, axis, pairs + [(high, low) for low, high in pairs])  13.9 us
    pallas_call x1, Pallas kernels, on_device(): pl.pallas_call(steps_and_remap, out_shape=(jax.ShapeDtypeStruct((9, N, N,...  6.31 us
    pallas_call x1, Pallas kernels, on_device(): pl.pallas_call(gather, out_shape=jax.ShapeDtypeStruct((9, SLOTS, W), f32)...  3.86 us
    pallas_call x1, Pallas kernels, on_device(): pl.pallas_call(bring, out_shape=jax.ShapeDtypeStruct((READY * 2 * N, W, W...  2.31 us
  transfers between devices with their start and end apart: 5, of which 0 were waited for; matrix products, arithmetic and copies ran while one was open for 2% of the time, Pallas kernels for 4%

profile of v5, /device:TPU:1, one launch (start us, length us, event | category | flops | bytes accessed | tf_op | source)
XLA Modules:
  0.0 88.8 jit_solution(2155698730814827567)
XLA Ops:
  0.6 0.0 copy-start.4
  0.6 0.0 copy-start.5
  0.7 1.2 %pack_cut.1 = (f32[34,16,128]{2,1,0:T(8,128)S(1)}, f32[34,16,128]{2,1,0:T(8,128)S(1)}) custom-call(s32[16,16]{1,0:T(8,128)} %flags_ref.1, f32[16,16]{1,0:T(8,128)} %yield_ref.1, f32[9,16,16,128]{3,2,1,0:T(8,128)} %state_ref.3, f32[16,16,128]{2,1,0:T(8,128)} %density_ref.3), custom_call_target="tpu_custom_call" | custom-call | tf_op jit(solution)/shard_map/pack_cut/pallas_call | solution.py:464
  1.9 0.7 collective-permute-start
  2.6 4.6 %collective-permute-start.1 = (f32[34,16,128]{2,1,0:T(8,128)S(1)}, f32[34,16,128]{2,1,0:T(8,128)S(1)}, u32[]{:S(2)}, u32[]{:S(2)}) collective-permute-start(f32[34,16,128]{2,1,0:T(8,128)S(1)} %get-tuple-element.14), channel_id=1, source_target_pairs={{0,8},{16,24},{32,40},{48,56},{64,72},{80,88},{96,104},{112,120},{... | collective-permute-start | bytes 835592 | tf_op jit(solution)/shard_map/ppermute | solution.py:443
  7.1 1.6 %pack_beside.1 = (f32[560,128]{1,0:T(8,128)S(1)}, f32[560,128]{1,0:T(8,128)S(1)}) custom-call(s32[16,16]{1,0:T(8,128)} %flags_ref.1, f32[16,16]{1,0:T(8,128)} %yield_ref.1, f32[9,16,16,128]{3,2,1,0:T(8,128)} %state_ref.3, f32[16,16,128]{2,1,0:T(8,128)} %density_ref.3), custom_call_target="tpu_custom_call" | custom-call | tf_op jit(solution)/shard_map/pack_beside/pallas_call | solution.py:479
  8.7 4.7 %collective-permute-start.2 = (f32[560,128]{1,0:T(8,128)S(1)}, f32[560,128]{1,0:T(8,128)S(1)}, u32[]{:S(2)}, u32[]{:S(2)}) collective-permute-start(f32[560,128]{1,0:T(8,128)S(1)} %get-tuple-element.17), channel_id=1, source_target_pairs={{1,2},{3,4},{5,6},{2,1},{4,3},{6,5},{9,10},{11,12},{13,14},{10,9},... | collective-permute-start | bytes 860168 | tf_op jit(solution)/shard_map/ppermute | solution.py:443
  13.4 0.8 copy.10
  14.2 0.2 fusion.2
  14.5 0.0 copy-done.4
  14.5 0.2 fusion.1
  14.7 0.0 copy-done.5
  14.8 0.0 collective-permute-done.cut_one_ref
  14.8 0.0 collective-permute-done.1.cut_two_ref
  14.8 0.1 pack_corners.1
  14.9 0.1 collective-permute-start.4
  15.0 0.4 fusion.4
  15.4 3.9 %collective-permute-start.3 = (f32[104,128]{1,0:T(8,128)S(1)}, f32[104,128]{1,0:T(8,128)S(1)}, u32[]{:S(2)}, u32[]{:S(2)}) collective-permute-start(f32[104,128]{1,0:T(8,128)S(1)} %get-tuple-element.19), channel_id=1, source_target_pairs={{1,2},{3,4},{5,6},{2,1},{4,3},{6,5},{9,10},{11,12},{13,14},{10,9},... | collective-permute-start | bytes 159752 | tf_op jit(solution)/shard_map/ppermute | solution.py:443
  19.3 0.0 copy-start
  19.4 0.0 copy-start.1
  19.4 0.0 copy-start.2
  19.4 0.0 copy-start.3
  19.4 2.3 %bring.1.ready_ref = bf16[128,128,128]{2,1,0:T(8,128)(2,1)S(1)} custom-call(bf16[512,128,128]{2,1,0:T(8,128)(2,1)} %weights_ref.2), custom_call_target="tpu_custom_call" | custom-call | bytes 4194304 | tf_op jit(solution)/shard_map/bring/pallas_call | solution.py:507
  21.7 0.0 collective-permute-done.2.beside_one_ref
  21.7 0.0 collective-permute-done.3.corner_one_ref
  21.7 0.0 collective-permute-done.4.side_two_ref
  21.7 0.1 copy-done
  21.9 0.0 copy-done.1
  21.9 0.0 copy-done.2
  21.9 0.0 copy-done.3
  21.9 6.3 %steps_and_remap.1 = (f32[9,16,16,128]{3,2,1,0:T(8,128)}, f32[896,8,128]{2,1,0:T(8,128)S(1)}) custom-call(s32[512]{0:T(512)S(1)} %multiply_add_fusion.place_ref, s32[16,16]{1,0:T(8,128)S(1)} %copy-done.2, f32[16,16]{1,0:T(8,128)S(1)} %copy-done.3, f32[9,16,16,128]{3,2,1,0:T(8,128)S(1)} %copy-done, f32[16,16,128]{2,1,0:T(8,128)S(1)} %copy-done.1, ...), custom_call_target="tpu_custom_call" | custom-call | tf_op jit(solution)/shard_map/steps_and_remap/pallas_call | solution.py:534
  28.2 56.8 %all_to_all.5 = f32[896,8,128]{2,1,0:T(8,128)S(1)} all-to-all(f32[896,8,128]{2,1,0:T(8,128)S(1)} %get-tuple-element.23), channel_id=1, replica_groups=mesh['cut'=16,'depth'=8] {'cut','depth'}, dimensions={0} | all-to-all | bytes 7340032 | tf_op jit(solution)/shard_map/all_to_all | solution.py:571
  85.0 3.9 %gather.1 = f32[9,256,128]{2,1,0:T(8,128)} custom-call(f32[128,7,8,128]{3,2,1,0:T(8,128)S(1)} %bitcast.14), custom_call_target="tpu_custom_call" | custom-call | tf_op jit(solution)/shard_map/gather/pallas_call | solution.py:572
  (8 shorter events, 0.1 us)
Async XLA Ops:
  0.6 13.9 %copy-start.4 = (s32[512,1]{0,1:T(1,128)S(1)}, s32[512,1]{0,1:T(1,128)}, u32[]{:S(2)}) copy-start(s32[512,1]{0,1:T(1,128)} %param.12) | copy-start | bytes 6148
  0.6 14.1 %copy-start.5 = (s32[512]{0:T(512)S(1)}, s32[512]{0:T(512)}, u32[]{:S(2)}) copy-start(s32[512]{0:T(512)} %param.13) | copy-start | bytes 6148
  1.9 12.9 %collective-permute-start = (f32[34,16,128]{2,1,0:T(8,128)S(1)}, f32[34,16,128]{2,1,0:T(8,128)S(1)}, u32[]{:S(2)}, u32[]{:S(2)}) collective-permute-start(f32[34,16,128]{2,1,0:T(8,128)S(1)} %get-tuple-element.13), channel_id=1, source_target_pairs={{8,16},{24,32},{40,48},{56,64},{72,80},{88,96},{104,112},{16,8},{3... | collective-permute-start | bytes 835592 | tf_op jit(solution)/shard_map/ppermute | solution.py:443
  2.6 12.2 %collective-permute-start.1 = (f32[34,16,128]{2,1,0:T(8,128)S(1)}, f32[34,16,128]{2,1,0:T(8,128)S(1)}, u32[]{:S(2)}, u32[]{:S(2)}) collective-permute-start(f32[34,16,128]{2,1,0:T(8,128)S(1)} %get-tuple-element.14), channel_id=1, source_target_pairs={{0,8},{16,24},{32,40},{48,56},{64,72},{80,88},{96,104},{112,120},{... | collective-permute-start | bytes 835592 | tf_op jit(solution)/shard_map/ppermute | solution.py:443
  8.7 13.0 %collective-permute-start.2 = (f32[560,128]{1,0:T(8,128)S(1)}, f32[560,128]{1,0:T(8,128)S(1)}, u32[]{:S(2)}, u32[]{:S(2)}) collective-permute-start(f32[560,128]{1,0:T(8,128)S(1)} %get-tuple-element.17), channel_id=1, source_target_pairs={{1,2},{3,4},{5,6},{2,1},{4,3},{6,5},{9,10},{11,12},{13,14},{10,9},... | collective-permute-start | bytes 860168 | tf_op jit(solution)/shard_map/ppermute | solution.py:443
  14.9 6.9 %collective-permute-start.4 = (f32[664,128]{1,0:T(8,128)S(1)}, f32[664,128]{1,0:T(8,128)S(1)}, u32[]{:S(2)}, u32[]{:S(2)}) collective-permute-start(f32[664,128]{1,0:T(8,128)S(1)} %get-tuple-element.20), channel_id=1, source_target_pairs={{0,1},{2,3},{4,5},{6,7},{1,0},{3,2},{5,4},{7,6},{8,9},{10,11},{12,... | collective-permute-start | bytes 1019912 | tf_op jit(solution)/shard_map/ppermute | solution.py:443
  15.4 6.3 %collective-permute-start.3 = (f32[104,128]{1,0:T(8,128)S(1)}, f32[104,128]{1,0:T(8,128)S(1)}, u32[]{:S(2)}, u32[]{:S(2)}) collective-permute-start(f32[104,128]{1,0:T(8,128)S(1)} %get-tuple-element.19), channel_id=1, source_target_pairs={{1,2},{3,4},{5,6},{2,1},{4,3},{6,5},{9,10},{11,12},{13,14},{10,9},... | collective-permute-start | bytes 159752 | tf_op jit(solution)/shard_map/ppermute | solution.py:443
  19.3 2.5 %copy-start = (f32[9,16,16,128]{3,2,1,0:T(8,128)S(1)}, f32[9,16,16,128]{3,2,1,0:T(8,128)}, u32[]{:S(2)}) copy-start(f32[9,16,16,128]{3,2,1,0:T(8,128)} %state_ref.3) | copy-start | bytes 3538948
  19.4 2.5 %copy-start.1 = (f32[16,16,128]{2,1,0:T(8,128)S(1)}, f32[16,16,128]{2,1,0:T(8,128)}, u32[]{:S(2)}) copy-start(f32[16,16,128]{2,1,0:T(8,128)} %density_ref.3) | copy-start | bytes 393220
  19.4 2.5 %copy-start.2 = (s32[16,16]{1,0:T(8,128)S(1)}, s32[16,16]{1,0:T(8,128)}, u32[]{:S(2)}) copy-start(s32[16,16]{1,0:T(8,128)} %flags_ref.1) | copy-start | bytes 3076
  19.4 2.5 %copy-start.3 = (f32[16,16]{1,0:T(8,128)S(1)}, f32[16,16]{1,0:T(8,128)}, u32[]{:S(2)}) copy-start(f32[16,16]{1,0:T(8,128)} %yield_ref.1) | copy-start | bytes 3076

commit v6 on v5

--- a/solution.py
+++ b/solution.py
@@ -495,6 +495,20 @@
         (beside_one, beside_two, crossing_weights)
     )
     beside_one = exchange(beside_one, "depth", 1)
+    owners = new_owner[:, 0]
+    hits = (owners[:, None] == jnp.arange(DEV, dtype=jnp.int32)[None, :]).astype(jnp.int32)
+    rank = jnp.sum((jnp.cumsum(hits, 0) - hits) * hits, 1)
+    place = owners * 8 + rank
+    by_rank = jnp.where(
+        rank[:, None] == jnp.arange(W, dtype=jnp.int32)[None, :], new_slot[:, None] + 1, 0
+    )
+    labels = lax.dot_general(
+        hits.astype(jnp.bfloat16),
+        by_rank.astype(jnp.bfloat16),
+        (((0,), (0,)), ((), ())),
+        preferred_element_type=f32,
+    )
+    cut_one, cut_two, labels, place = lax.optimization_barrier((cut_one, cut_two, labels, place))
     one, two = pl.pallas_call(
         pack_corners,
         out_shape=both((CORNER_ROWS,))[:1] + both((SIDE_ROWS,))[:1],
@@ -516,20 +530,6 @@
         ),
         name="bring",
     )(stay(weights))
-
-    owners = new_owner[:, 0]
-    hits = (owners[:, None] == jnp.arange(DEV, dtype=jnp.int32)[None, :]).astype(jnp.int32)
-    rank = jnp.sum((jnp.cumsum(hits, 0) - hits) * hits, 1)
-    place = owners * 8 + rank
-    by_rank = jnp.where(
-        rank[:, None] == jnp.arange(W, dtype=jnp.int32)[None, :], new_slot[:, None] + 1, 0
-    )
-    labels = lax.dot_general(
-        hits.astype(jnp.bfloat16),
-        by_rank.astype(jnp.bfloat16),
-        (((0,), (0,)), ((), ())),
-        preferred_element_type=f32,
-    )
 
     state_after, outgoing = pl.pallas_call(
         steps_and_remap,

time: 89.2 us -> 91.9 us (1.030)
  other arithmetic: 0.5 us -> 2.54 us
  waiting for transfers between devices: 0.01 us -> 1.74 us
  starting transfers between devices: 13.9 us -> 12.5 us
    ppermute x5, waiting for transfers between devices: 0.01 us -> 1.74 us  [exchange(): return lax.ppermute(x, axis, pairs + [(high, low) for low, high in pairs])]
    ppermute x5, starting transfers between devices: 13.9 us -> 12.5 us  [exchange(): return lax.ppermute(x, axis, pairs + [(high, low) for low, high in pairs])]
  transfers between devices with their start and end apart: 5 -> 5, of which waited for: 0 -> 2; matrix products, arithmetic and copies ran while one was open for 2% -> 4% of each run, Pallas kernels for 4% -> 4%
where the time goes in v6:
time: 91.9 us; the launch traced here: 91.5 us
  blocking collectives  57.3 us (62%)
  Pallas kernels  15.3 us (17%)
  starting transfers between devices  12.5 us (14%)
  other arithmetic  2.54 us (3%)
  waiting for transfers between devices  1.74 us (2%)
    all_to_all x1, blocking collectives, on_device(): lax.all_to_all(outgoing, ('cut', 'depth'), split_axis=0, concat_axis=0, t...  57.3 us
    ppermute x5, starting transfers between devices, exchange(): return lax.ppermute(x, axis, pairs + [(high, low) for low, high in pairs])  12.5 us
    pallas_call x1, Pallas kernels, on_device(): pl.pallas_call(steps_and_remap, out_shape=(jax.ShapeDtypeStruct((9, N, N,...  6.33 us
    pallas_call x1, Pallas kernels, on_device(): pl.pallas_call(gather, out_shape=jax.ShapeDtypeStruct((9, SLOTS, W), f32)...  3.9 us
    pallas_call x1, Pallas kernels, on_device(): pl.pallas_call(bring, out_shape=jax.ShapeDtypeStruct((READY * 2 * N, W, W...  2.22 us
  transfers between devices with their start and end apart: 5, of which 2 were waited for; matrix products, arithmetic and copies ran while one was open for 4% of the time, Pallas kernels for 4%

profile of v6, /device:TPU:1, one launch (start us, length us, event | category | flops | bytes accessed | tf_op | source)
XLA Modules:
  0.0 91.5 jit_solution(2799907471969476403)
XLA Ops:
  0.6 0.0 copy-start.4
  0.6 1.2 %pack_cut.1 = (f32[34,16,128]{2,1,0:T(8,128)S(1)}, f32[34,16,128]{2,1,0:T(8,128)S(1)}) custom-call(s32[16,16]{1,0:T(8,128)} %flags_ref.1, f32[16,16]{1,0:T(8,128)} %yield_ref.1, f32[9,16,16,128]{3,2,1,0:T(8,128)} %state_ref.3, f32[16,16,128]{2,1,0:T(8,128)} %density_ref.3), custom_call_target="tpu_custom_call" | custom-call | tf_op jit(solution)/shard_map/pack_cut/pallas_call | solution.py:464
  1.9 0.7 collective-permute-start
  2.6 4.6 %collective-permute-start.1 = (f32[34,16,128]{2,1,0:T(8,128)S(1)}, f32[34,16,128]{2,1,0:T(8,128)S(1)}, u32[]{:S(2)}, u32[]{:S(2)}) collective-permute-start(f32[34,16,128]{2,1,0:T(8,128)S(1)} %get-tuple-element.18), channel_id=1, source_target_pairs={{0,8},{16,24},{32,40},{48,56},{64,72},{80,88},{96,104},{112,120},{... | collective-permute-start | bytes 835592 | tf_op jit(solution)/shard_map/ppermute | solution.py:443
  7.1 0.8 copy.10
  7.9 0.2 fusion.2
  8.2 0.9 fusion.1
  9.1 0.7 multiply_add_fusion.place_ref
  9.8 0.7 broadcast_add_fusion.1
  10.5 1.6 %pack_beside.1 = (f32[560,128]{1,0:T(8,128)S(1)}, f32[560,128]{1,0:T(8,128)S(1)}) custom-call(s32[16,16]{1,0:T(8,128)} %flags_ref.1, f32[16,16]{1,0:T(8,128)} %yield_ref.1, f32[9,16,16,128]{3,2,1,0:T(8,128)} %state_ref.3, f32[16,16,128]{2,1,0:T(8,128)} %density_ref.3), custom_call_target="tpu_custom_call" | custom-call | tf_op jit(solution)/shard_map/pack_beside/pallas_call | solution.py:479
  12.1 0.0 copy-done.4
  12.1 0.4 fusion.4
  12.5 0.0 collective-permute-done.cut_one_ref
  12.6 0.6 collective-permute-done.1.cut_two_ref
  13.2 0.1 pack_corners.1
  13.3 1.6 %collective-permute-start.4 = (f32[664,128]{1,0:T(8,128)S(1)}, f32[664,128]{1,0:T(8,128)S(1)}, u32[]{:S(2)}, u32[]{:S(2)}) collective-permute-start(f32[664,128]{1,0:T(8,128)S(1)} %get-tuple-element.27), channel_id=1, source_target_pairs={{0,1},{2,3},{4,5},{6,7},{1,0},{3,2},{5,4},{7,6},{8,9},{10,11},{12,... | collective-permute-start | bytes 1019912 | tf_op jit(solution)/shard_map/ppermute | solution.py:443
  14.9 3.4 %collective-permute-start.2 = (f32[560,128]{1,0:T(8,128)S(1)}, f32[560,128]{1,0:T(8,128)S(1)}, u32[]{:S(2)}, u32[]{:S(2)}) collective-permute-start(f32[560,128]{1,0:T(8,128)S(1)} %get-tuple-element.24), channel_id=1, source_target_pairs={{1,2},{3,4},{5,6},{2,1},{4,3},{6,5},{9,10},{11,12},{13,14},{10,9},... | collective-permute-start | bytes 860168 | tf_op jit(solution)/shard_map/ppermute | solution.py:443
  18.3 0.0 copy-start
  18.4 0.0 copy-start.1
  18.4 0.0 copy-start.2
  18.4 0.0 copy-start.3
  18.4 2.2 %collective-permute-start.3 = (f32[104,128]{1,0:T(8,128)S(1)}, f32[104,128]{1,0:T(8,128)S(1)}, u32[]{:S(2)}, u32[]{:S(2)}) collective-permute-start(f32[104,128]{1,0:T(8,128)S(1)} %get-tuple-element.26), channel_id=1, source_target_pairs={{1,2},{3,4},{5,6},{2,1},{4,3},{6,5},{9,10},{11,12},{13,14},{10,9},... | collective-permute-start | bytes 159752 | tf_op jit(solution)/shard_map/ppermute | solution.py:443
  20.6 2.2 %bring.1.ready_ref = bf16[128,128,128]{2,1,0:T(8,128)(2,1)S(1)} custom-call(bf16[512,128,128]{2,1,0:T(8,128)(2,1)} %weights_ref.2), custom_call_target="tpu_custom_call" | custom-call | bytes 4194304 | tf_op jit(solution)/shard_map/bring/pallas_call | solution.py:521
  22.9 0.0 collective-permute-done.2.beside_one_ref
  22.9 1.1 %collective-permute-done.3.corner_one_ref = f32[104,128]{1,0:T(8,128)S(1)} collective-permute-done((f32[104,128]{1,0:T(8,128)S(1)}, f32[104,128]{1,0:T(8,128)S(1)}, u32[]{:S(2)}, u32[]{:S(2)}) %collective-permute-start.3) | collective-permute-done | bytes 53280 | tf_op jit(solution)/shard_map/ppermute | solution.py:443
  24.0 0.0 collective-permute-done.4.side_two_ref
  24.0 0.0 copy-done
  24.0 0.0 copy-done.1
  24.0 0.0 copy-done.2
  24.0 0.0 copy-done.3
  24.0 6.3 %steps_and_remap.1 = (f32[9,16,16,128]{3,2,1,0:T(8,128)}, f32[896,8,128]{2,1,0:T(8,128)S(1)}) custom-call(s32[512]{0:T(512)S(1)} %multiply_add_fusion.place_ref, s32[16,16]{1,0:T(8,128)S(1)} %copy-done.2, f32[16,16]{1,0:T(8,128)S(1)} %copy-done.3, f32[9,16,16,128]{3,2,1,0:T(8,128)S(1)} %copy-done, f32[16,16,128]{2,1,0:T(8,128)S(1)} %copy-done.1, ...), custom_call_target="tpu_custom_call" | custom-call | tf_op jit(solution)/shard_map/steps_and_remap/pallas_call | solution.py:534
  30.3 57.3 %all_to_all.5 = f32[896,8,128]{2,1,0:T(8,128)S(1)} all-to-all(f32[896,8,128]{2,1,0:T(8,128)S(1)} %get-tuple-element.31), channel_id=1, replica_groups=mesh['cut'=16,'depth'=8] {'cut','depth'}, dimensions={0} | all-to-all | bytes 7340032 | tf_op jit(solution)/shard_map/all_to_all | solution.py:571
  87.6 3.9 %gather.1 = f32[9,256,128]{2,1,0:T(8,128)} custom-call(f32[128,7,8,128]{3,2,1,0:T(8,128)S(1)} %bitcast.14), custom_call_target="tpu_custom_call" | custom-call | tf_op jit(solution)/shard_map/gather/pallas_call | solution.py:572
  (6 shorter events, 0.1 us)
Async XLA Ops:
  0.6 11.5 %copy-start.4 = (s32[512,1]{0,1:T(1,128)S(1)}, s32[512,1]{0,1:T(1,128)}, u32[]{:S(2)}) copy-start(s32[512,1]{0,1:T(1,128)} %param.12) | copy-start | bytes 6148
  1.9 10.7 %collective-permute-start = (f32[34,16,128]{2,1,0:T(8,128)S(1)}, f32[34,16,128]{2,1,0:T(8,128)S(1)}, u32[]{:S(2)}, u32[]{:S(2)}) collective-permute-start(f32[34,16,128]{2,1,0:T(8,128)S(1)} %get-tuple-element.17), channel_id=1, source_target_pairs={{8,16},{24,32},{40,48},{56,64},{72,80},{88,96},{104,112},{16,8},{3... | collective-permute-start | bytes 835592 | tf_op jit(solution)/shard_map/ppermute | solution.py:443
  2.6 10.6 %collective-permute-start.1 = (f32[34,16,128]{2,1,0:T(8,128)S(1)}, f32[34,16,128]{2,1,0:T(8,128)S(1)}, u32[]{:S(2)}, u32[]{:S(2)}) collective-permute-start(f32[34,16,128]{2,1,0:T(8,128)S(1)} %get-tuple-element.18), channel_id=1, source_target_pairs={{0,8},{16,24},{32,40},{48,56},{64,72},{80,88},{96,104},{112,120},{... | collective-permute-start | bytes 835592 | tf_op jit(solution)/shard_map/ppermute | solution.py:443
  13.3 10.7 %collective-permute-start.4 = (f32[664,128]{1,0:T(8,128)S(1)}, f32[664,128]{1,0:T(8,128)S(1)}, u32[]{:S(2)}, u32[]{:S(2)}) collective-permute-start(f32[664,128]{1,0:T(8,128)S(1)} %get-tuple-element.27), channel_id=1, source_target_pairs={{0,1},{2,3},{4,5},{6,7},{1,0},{3,2},{5,4},{7,6},{8,9},{10,11},{12,... | collective-permute-start | bytes 1019912 | tf_op jit(solution)/shard_map/ppermute | solution.py:443
  14.9 8.0 %collective-permute-start.2 = (f32[560,128]{1,0:T(8,128)S(1)}, f32[560,128]{1,0:T(8,128)S(1)}, u32[]{:S(2)}, u32[]{:S(2)}) collective-permute-start(f32[560,128]{1,0:T(8,128)S(1)} %get-tuple-element.24), channel_id=1, source_target_pairs={{1,2},{3,4},{5,6},{2,1},{4,3},{6,5},{9,10},{11,12},{13,14},{10,9},... | collective-permute-start | bytes 860168 | tf_op jit(solution)/shard_map/ppermute | solution.py:443
  18.3 5.6 %copy-start = (f32[9,16,16,128]{3,2,1,0:T(8,128)S(1)}, f32[9,16,16,128]{3,2,1,0:T(8,128)}, u32[]{:S(2)}) copy-start(f32[9,16,16,128]{3,2,1,0:T(8,128)} %state_ref.3) | copy-start | bytes 3538948
  18.4 5.6 %copy-start.1 = (f32[16,16,128]{2,1,0:T(8,128)S(1)}, f32[16,16,128]{2,1,0:T(8,128)}, u32[]{:S(2)}) copy-start(f32[16,16,128]{2,1,0:T(8,128)} %density_ref.3) | copy-start | bytes 393220
  18.4 5.6 %copy-start.2 = (s32[16,16]{1,0:T(8,128)S(1)}, s32[16,16]{1,0:T(8,128)}, u32[]{:S(2)}) copy-start(s32[16,16]{1,0:T(8,128)} %flags_ref.1) | copy-start | bytes 3076
  18.4 5.6 %copy-start.3 = (f32[16,16]{1,0:T(8,128)S(1)}, f32[16,16]{1,0:T(8,128)}, u32[]{:S(2)}) copy-start(f32[16,16]{1,0:T(8,128)} %yield_ref.1) | copy-start | bytes 3076
  18.4 5.6 %collective-permute-start.3 = (f32[104,128]{1,0:T(8,128)S(1)}, f32[104,128]{1,0:T(8,128)S(1)}, u32[]{:S(2)}, u32[]{:S(2)}) collective-permute-start(f32[104,128]{1,0:T(8,128)S(1)} %get-tuple-element.26), channel_id=1, source_target_pairs={{1,2},{3,4},{5,6},{2,1},{4,3},{6,5},{9,10},{11,12},{13,14},{10,9},... | collective-permute-start | bytes 159752 | tf_op jit(solution)/shard_map/ppermute | solution.py:443
